TPU v7x, 32 devices: a whole 2x2x4 slice. The times are simulated.
32 devices in a mesh: bx: 4 (over y, core), by: 8 (over z, x).
Axes of the slice: x: 2, y: 2, z: 4, core: 2. Of those that a mesh axis runs over, the one named last changes fastest.
Arguments:
- point_box: int32 [65536, 1], P(('bx', 'by')), may hold values from 0 to 31; in each aligned block of 2048 rows (0 to 2047, 2048 to 4095, ...) at most 128 rows name the same one
- point_offset: int32 [2, 65536], P(None, ('bx', 'by')), may hold values from 0 to 2047
- point_value: float32 [2, 65536], P(None, ('bx', 'by')), may hold values from -0.0625 to 0.0625
- coef: int32 [4], replicated, may hold values from 0 to 31
Outputs:
- weights: float32 [2, 64, 32768], P(None, None, ('bx', 'by'))
Inputs may be any that keep to these rules, and one draw needn't show every extreme that they name: `point_box`: the 2048 points of one device name any one box at most 128 times, a bound that some block reaches.
All inputs are finite; a program needn't handle non-finite values.
Results may differ from a plain program's by a relative error of at most 0.0012.
Values sent between devices are 32-bit elements; how exact they have to be, the bound alone decides.
A program may use at most 64 MiB of HBM per device.

v0:
```python
import jax
import jax.numpy as jnp
import numpy as np
from jax import lax
from jax.sharding import PartitionSpec as P

N = 16384
ORDER = 8
TGT1 = 32
TGT2 = 32
BLOCK = 256


def from_partner(value, axis, distance):
    return lax.ppermute(value, axis, [(i, i ^ 1 << distance) for i in range(lax.axis_size(axis))])


def node_table():
    counting = np.arange(ORDER) * 1.0
    return 0.5 - 0.5 * np.cos(np.pi * (2.0 * counting + 1.0) / (2.0 * ORDER))


def lagrange(coords):
    nodes = node_table()
    columns = []
    for target in range(ORDER):
        factor = jnp.ones_like(coords)
        for source in range(ORDER):
            if source != target:
                factor = factor * (
                    (coords - float(nodes[source])) * float(1.0 / (nodes[target] - nodes[source]))
                )
        columns.append(factor)
    return jnp.stack(columns, axis=-1)


def child_matrix(side):
    nodes = node_table()
    points = 0.5 * (side + nodes)
    rows_all = []
    for target in range(ORDER):
        factor = np.ones(ORDER)
        for source in range(ORDER):
            if source != target:
                factor = factor * (points - nodes[source]) / (nodes[target] - nodes[source])
        rows_all.append(factor)
    return jnp.asarray(np.stack(rows_all), dtype=jnp.float32)


def phases(tgt_first, tgt_second, freq_first, freq_second, coef):
    scaled = coef.astype(jnp.float32)
    wave = jnp.sin(128.0 * jnp.pi * (tgt_first + tgt_second))
    speed_first = (32.0 + scaled[0] + scaled[1] * wave) / 4096.0
    speed_second = (32.0 + scaled[2] + scaled[3] * wave) / 4096.0
    kfirst = freq_first[:, None]
    ksecond = freq_second[:, None]
    total = (
        tgt_first * kfirst
        + tgt_second * ksecond
        + jnp.sqrt(1.0 + (speed_first * kfirst) ** 2 + (speed_second * ksecond) ** 2)
    )
    fraction = total - jnp.floor(total)
    return (jnp.cos(2.0 * jnp.pi * fraction), jnp.sin(2.0 * jnp.pi * fraction))


def grid_nodes(corner_first, width_first, corner_second, width_second):
    nodes = jnp.asarray(node_table(), dtype=jnp.float32)
    along_first = corner_first + width_first * nodes
    along_second = corner_second + width_second * nodes
    return (
        jnp.broadcast_to(along_first[:, None], (ORDER, ORDER)).reshape(-1),
        jnp.broadcast_to(along_second[None, :], (ORDER, ORDER)).reshape(-1),
    )


def tgt_axis(index, merged, count, boxes):
    code = jnp.zeros((), jnp.int32)
    for bit in range(merged):
        code = code + (index >> bit & 1) * 2 ** (merged - 1 - bit)
    place = jnp.arange(count, dtype=jnp.int32) * 2**merged + code
    return (place.astype(jnp.float32) + 0.5) * (boxes / (N * 2.0**merged))


def centers(index_x, index_y, merged_x, merged_y, boxes_x, boxes_y):
    first = tgt_axis(index_x, merged_x, TGT1, boxes_x)
    second = tgt_axis(index_y, merged_y, TGT2, boxes_y)
    return (
        jnp.broadcast_to(first[:, None], (TGT1, TGT2)).reshape(-1),
        jnp.broadcast_to(second[None, :], (TGT1, TGT2)).reshape(-1),
    )


def leaf_terms(
    columns, corner_first, width_first, corner_second, width_second, tgt_first, tgt_second, coef
):
    cosine, sine = phases(tgt_first, tgt_second, columns[0], columns[1], coef)
    real_in = columns[2][:, None]
    imag_in = columns[3][:, None]
    real_part = cosine * real_in - sine * imag_in
    imag_part = cosine * imag_in + sine * real_in
    basis_first = lagrange((columns[0] - corner_first) / width_first)
    basis_second = lagrange((columns[1] - corner_second) / width_second)
    basis = (basis_first[:, :, None] * basis_second[:, None, :]).reshape(
        columns.shape[1], ORDER * ORDER
    )
    dims = (((0,), (0,)), ((), ()))
    real_sum = lax.dot_general(
        basis, real_part, dims, precision=lax.Precision.HIGHEST, preferred_element_type=jnp.float32
    )
    imag_sum = lax.dot_general(
        basis, imag_part, dims, precision=lax.Precision.HIGHEST, preferred_element_type=jnp.float32
    )
    return (real_sum, imag_sum)


def shift_back(real_sum, imag_sum, node_first, node_second, tgt_first, tgt_second, coef):
    cosine, sine = phases(tgt_first, tgt_second, node_first, node_second, coef)
    return jnp.stack([cosine * real_sum + sine * imag_sum, cosine * imag_sum - sine * real_sum])


def merge_box(
    first_w, second_w, tgt_first, tgt_second, along, corner_d, width_d, corner_o, width_o, coef
):
    spreads = []
    for side, child in ((0, first_w), (1, second_w)):
        start = corner_d + side * width_d
        if along == 1:
            node_first, node_second = grid_nodes(start, width_d, corner_o, width_o)
        else:
            node_first, node_second = grid_nodes(corner_o, width_o, start, width_d)
        cosine, sine = phases(tgt_first, tgt_second, node_first, node_second, coef)
        lifted = jnp.stack(
            [cosine * child[0] - sine * child[1], cosine * child[1] + sine * child[0]]
        )
        lifted = lifted.reshape(2, ORDER, ORDER, -1)
        table = child_matrix(side)
        if along == 1:
            spreads.append(
                jnp.einsum("ts,rsuk->rtuk", table, lifted, precision=lax.Precision.HIGHEST)
            )
        else:
            spreads.append(
                jnp.einsum("us,rtsk->rtuk", table, lifted, precision=lax.Precision.HIGHEST)
            )
    total = (spreads[0] + spreads[1]).reshape(2, ORDER * ORDER, -1)
    if along == 1:
        node_first, node_second = grid_nodes(corner_d, 2.0 * width_d, corner_o, width_o)
    else:
        node_first, node_second = grid_nodes(corner_o, width_o, corner_d, 2.0 * width_d)
    return shift_back(total[0], total[1], node_first, node_second, tgt_first, tgt_second, coef)


def merge_first(holding, partner, index_x, row_y, level, boxes_x, boxes_y, coef):
    width_first = N // boxes_x
    width_second = N // boxes_y
    flag = index_x >> level & 1 == 0
    first_w = jnp.where(flag, holding, partner)
    second_w = jnp.where(flag, partner, holding)
    tgt_first, tgt_second = centers(index_x, row_y, level + 1, level, boxes_x, boxes_y)
    corner_d = ((index_x >> level + 1) * (width_first * 2 ** (level + 1))).astype(jnp.float32)
    corner_o = ((row_y >> level) * (width_second * 2**level)).astype(jnp.float32)
    return merge_box(
        first_w,
        second_w,
        tgt_first,
        tgt_second,
        1,
        corner_d,
        float(width_first * 2**level),
        corner_o,
        float(width_second * 2**level),
        coef,
    )


def merge_second(holding, partner, index_x, index_y, level, boxes_x, boxes_y, coef):
    width_first = N // boxes_x
    width_second = N // boxes_y
    flag = index_y >> level & 1 == 0
    first_w = jnp.where(flag, holding, partner)
    second_w = jnp.where(flag, partner, holding)
    tgt_first, tgt_second = centers(index_x, index_y, level + 1, level + 1, boxes_x, boxes_y)
    corner_d = ((index_y >> level + 1) * (width_second * 2 ** (level + 1))).astype(jnp.float32)
    corner_o = ((index_x >> level + 1) * (width_first * 2 ** (level + 1))).astype(jnp.float32)
    return merge_box(
        first_w,
        second_w,
        tgt_first,
        tgt_second,
        2,
        corner_d,
        float(width_second * 2**level),
        corner_o,
        float(width_first * 2 ** (level + 1)),
        coef,
    )


def pack_slots(box_ids, offsets, values, boxes_y, width_first, width_second, owners, slot_cap):
    ids = box_ids[:, 0]
    onehot = (ids[:, None] == jnp.arange(owners, dtype=jnp.int32)[None, :]).astype(jnp.int32)
    ranks = jnp.sum((jnp.cumsum(onehot, axis=0) - 1) * onehot, axis=1)
    freq_first = (ids // boxes_y * width_first + offsets[0]).astype(jnp.float32)
    freq_second = (ids % boxes_y * width_second + offsets[1]).astype(jnp.float32)
    stacked = jnp.stack([freq_first, freq_second, values[0], values[1]], axis=0)
    slot_of = ids * slot_cap + ranks
    blank = jnp.concatenate(
        [
            jnp.full((2, owners * slot_cap), -1.0, jnp.float32),
            jnp.zeros((2, owners * slot_cap), jnp.float32),
        ],
        axis=0,
    )
    filled = blank.at[:, slot_of].set(stacked)
    return filled.reshape(4, owners, slot_cap).transpose(1, 0, 2).reshape(owners, 4 * slot_cap)


def spread_columns(arrived):
    owners = arrived.shape[0]
    return arrived.reshape(owners, 4, -1).transpose(1, 0, 2).reshape(4, -1)


def trade_first(weights, level):
    return from_partner(weights, "bx", level)


def trade_second(weights, level):
    return from_partner(weights, "by", level)


def on_device(point_box, point_offset, point_value, coef):
    boxes_x = lax.axis_size("bx")
    boxes_y = lax.axis_size("by")
    owners = boxes_x * boxes_y
    slot_cap = 2 * point_box.shape[0] // owners
    width_first = N // boxes_x
    width_second = N // boxes_y
    index_x = lax.axis_index("bx")
    index_y = lax.axis_index("by")
    sent = pack_slots(
        point_box, point_offset, point_value, boxes_y, width_first, width_second, owners, slot_cap
    )
    arrived = lax.all_to_all(sent, ("bx", "by"), split_axis=0, concat_axis=0, tiled=True)
    columns = spread_columns(arrived)
    tgt_first, tgt_second = centers(index_x, index_y, 0, 0, boxes_x, boxes_y)
    slots = columns.shape[1]
    corner_first = (index_x * width_first).astype(jnp.float32)
    corner_second = (index_y * width_second).astype(jnp.float32)
    blocks = slots // BLOCK

    def add_block(number, totals):
        piece = lax.dynamic_slice_in_dim(columns, number * BLOCK, BLOCK, 1)
        real_sum, imag_sum = leaf_terms(
            piece,
            corner_first,
            float(width_first),
            corner_second,
            float(width_second),
            tgt_first,
            tgt_second,
            coef,
        )
        return (totals[0] + real_sum, totals[1] + imag_sum)

    empty = jnp.zeros((ORDER * ORDER, TGT1 * TGT2), jnp.float32)
    real_sum, imag_sum = lax.fori_loop(0, blocks, add_block, (empty, empty))
    node_first, node_second = grid_nodes(
        corner_first, float(width_first), corner_second, float(width_second)
    )
    holding = shift_back(real_sum, imag_sum, node_first, node_second, tgt_first, tgt_second, coef)
    first_level = 0
    for level in range(first_level, 2):
        partner = trade_first(holding, level)
        holding = merge_first(holding, partner, index_x, index_y, level, boxes_x, boxes_y, coef)
        partner = trade_second(holding, level)
        holding = merge_second(holding, partner, index_x, index_y, level, boxes_x, boxes_y, coef)
    return holding


def solution(mesh):
    in_specs = (P(("bx", "by"), None), P(None, ("bx", "by")), P(None, ("bx", "by")), P())
    out_specs = P(None, None, ("bx", "by"))
    return jax.shard_map(
        on_device, mesh=mesh, in_specs=in_specs, out_specs=out_specs, check_vma=False
    )
```

profile of v0, /device:TPU:0, one launch (start us, length us, event | category | flops | bytes accessed | tf_op | source)
XLA Modules:
  0.0 314.0 jit_solution(3579781578116448517)
XLA Ops:
  0.8 9.1 %reduce-window.6 = s32[32,16,128]{2,1,0:T(8,128)S(1)} reduce-window(s32[32,16,128]{2,1,0:T(8,128)S(1)} %fusion.114, s32[]{:T(128)} %constant.602.clone.1), window={size=1x1x128 pad=0_0x0_0x127_0}, to_apply=%region_0.0 | reduce-window | flops 8323072 | bytes 524292 | tf_op jit(solution)/shard_map/reduce-window
  11.3 1.5 copy-done
  12.8 6.4 %scatter_fusion = f32[4,4096]{0,1:T(8,128)S(1)} fusion(f32[4,4096]{0,1:T(8,128)S(1)} %copy-done, s32[2048]{0:T(1024)S(1)} %bitcast.242, f32[2048,4]{1,0:T(8,128)S(1)} %copy.45), kind=kCustom, calls=%fused_computation | custom fusion | bytes 106496 | tf_op jit(solution)/shard_map/scatter | solution.py:214
  20.5 7.5 %all-to-all-start = ((f32[32,1,512]{2,1,0:T(1,128)}), f32[32,1,512]{2,1,0:T(1,128)S(1)}, u32[]{:S(2)}, u32[]{:S(2)}) async-start(f32[32,1,512]{2,1,0:T(1,128)} %bitcast.15), calls=%async_computation | async-start | bytes 131072 | tf_op jit(solution)/shard_map/all_to_all | solution.py:243
  30.9 1.3 add_multiply_fusion.11
  32.2 2.8 all-to-all-done
  35.0 213.6 %while.22 = (s32[]{:T(128)}, f32[64,1024]{1,0:T(8,128)S(1)}, f32[64,1024]{1,0:T(8,128)S(1)}, f32[4,4096]{1,0:T(4,128)S(1)}, f32[]{:T(128)}, /*index=5*/f32[]{:T(...) while((s32[]{:T(128)}, f32[64,1024]{1,0:T(8,128)S(1)}, ...), condition=%wide.region_5.6_spmd.clone.clone.clone.clone, body=%wide.region_4.5_spmd.clone.clone.clone.clone.sunk | while | flops 411406848 | bytes 1233722 | solution.py:266
  36.1 1.5 add_multiply_fusion.17
  37.8 5.3 %convolution_add_fusion.9 = f32[64,1024]{1,0:T(8,128)S(1)} fusion(f32[256]{0:T(256)S(1)} %bitcast.250, f32[256]{0:T(256)S(1)} %bitcast.246, f32[1024]{0:T(1024)S(1)} %bitcast.238, f32[1024]{0:T(1024)S(1)} %bitcast.236, f32[256]{0:T(256)S(1)} %bitcast.248, f32[1024]{0:T(1024)S(1)} %mul.9761, f32[256]{0:T(256)S(1)} %bitcast.244, f32[1024]{0:T(1024)S(1)} %mul.9762, ...), kind=kOutput, calls=%fused_computation.5.clone.1 | convolution fusion | flops 205668352 | bytes 561153 | tf_op jit(solution)/shard_map/while/body/eval_jaxpr/dot_general | solution.py:110
  43.1 5.3 %convolution_add_fusion.8 = f32[64,1024]{1,0:T(8,128)S(1)} fusion(f32[256]{0:T(256)S(1)} %bitcast.251, f32[256]{0:T(256)S(1)} %bitcast.247, f32[1024]{0:T(1024)S(1)} %bitcast.239, f32[1024]{0:T(1024)S(1)} %bitcast.237, f32[256]{0:T(256)S(1)} %bitcast.249, f32[1024]{0:T(1024)S(1)} %mul.9761, f32[256]{0:T(256)S(1)} %bitcast.245, f32[1024]{0:T(1024)S(1)} %mul.9762, ...), kind=kOutput, calls=%fused_computation.6.clone.1 | convolution fusion | flops 205668352 | bytes 561153 | tf_op jit(solution)/shard_map/while/body/eval_jaxpr/dot_general | solution.py:107
  49.4 1.5 add_multiply_fusion.17
  51.1 5.3 %convolution_add_fusion.9 = f32[64,1024]{1,0:T(8,128)S(1)} fusion(f32[256]{0:T(256)S(1)} %bitcast.250, f32[256]{0:T(256)S(1)} %bitcast.246, f32[1024]{0:T(1024)S(1)} %bitcast.238, f32[1024]{0:T(1024)S(1)} %bitcast.236, f32[256]{0:T(256)S(1)} %bitcast.248, f32[1024]{0:T(1024)S(1)} %mul.9761, f32[256]{0:T(256)S(1)} %bitcast.244, f32[1024]{0:T(1024)S(1)} %mul.9762, ...), kind=kOutput, calls=%fused_computation.5.clone.1 | convolution fusion | flops 205668352 | bytes 561153 | tf_op jit(solution)/shard_map/while/body/eval_jaxpr/dot_general | solution.py:110
  56.4 5.3 %convolution_add_fusion.8 = f32[64,1024]{1,0:T(8,128)S(1)} fusion(f32[256]{0:T(256)S(1)} %bitcast.251, f32[256]{0:T(256)S(1)} %bitcast.247, f32[1024]{0:T(1024)S(1)} %bitcast.239, f32[1024]{0:T(1024)S(1)} %bitcast.237, f32[256]{0:T(256)S(1)} %bitcast.249, f32[1024]{0:T(1024)S(1)} %mul.9761, f32[256]{0:T(256)S(1)} %bitcast.245, f32[1024]{0:T(1024)S(1)} %mul.9762, ...), kind=kOutput, calls=%fused_computation.6.clone.1 | convolution fusion | flops 205668352 | bytes 561153 | tf_op jit(solution)/shard_map/while/body/eval_jaxpr/dot_general | solution.py:107
  62.8 1.5 add_multiply_fusion.17
  64.4 5.3 %convolution_add_fusion.9 = f32[64,1024]{1,0:T(8,128)S(1)} fusion(f32[256]{0:T(256)S(1)} %bitcast.250, f32[256]{0:T(256)S(1)} %bitcast.246, f32[1024]{0:T(1024)S(1)} %bitcast.238, f32[1024]{0:T(1024)S(1)} %bitcast.236, f32[256]{0:T(256)S(1)} %bitcast.248, f32[1024]{0:T(1024)S(1)} %mul.9761, f32[256]{0:T(256)S(1)} %bitcast.244, f32[1024]{0:T(1024)S(1)} %mul.9762, ...), kind=kOutput, calls=%fused_computation.5.clone.1 | convolution fusion | flops 205668352 | bytes 561153 | tf_op jit(solution)/shard_map/while/body/eval_jaxpr/dot_general | solution.py:110
  69.7 5.3 %convolution_add_fusion.8 = f32[64,1024]{1,0:T(8,128)S(1)} fusion(f32[256]{0:T(256)S(1)} %bitcast.251, f32[256]{0:T(256)S(1)} %bitcast.247, f32[1024]{0:T(1024)S(1)} %bitcast.239, f32[1024]{0:T(1024)S(1)} %bitcast.237, f32[256]{0:T(256)S(1)} %bitcast.249, f32[1024]{0:T(1024)S(1)} %mul.9761, f32[256]{0:T(256)S(1)} %bitcast.245, f32[1024]{0:T(1024)S(1)} %mul.9762, ...), kind=kOutput, calls=%fused_computation.6.clone.1 | convolution fusion | flops 205668352 | bytes 561153 | tf_op jit(solution)/shard_map/while/body/eval_jaxpr/dot_general | solution.py:107
  76.1 1.5 add_multiply_fusion.17
  77.8 5.3 %convolution_add_fusion.9 = f32[64,1024]{1,0:T(8,128)S(1)} fusion(f32[256]{0:T(256)S(1)} %bitcast.250, f32[256]{0:T(256)S(1)} %bitcast.246, f32[1024]{0:T(1024)S(1)} %bitcast.238, f32[1024]{0:T(1024)S(1)} %bitcast.236, f32[256]{0:T(256)S(1)} %bitcast.248, f32[1024]{0:T(1024)S(1)} %mul.9761, f32[256]{0:T(256)S(1)} %bitcast.244, f32[1024]{0:T(1024)S(1)} %mul.9762, ...), kind=kOutput, calls=%fused_computation.5.clone.1 | convolution fusion | flops 205668352 | bytes 561153 | tf_op jit(solution)/shard_map/while/body/eval_jaxpr/dot_general | solution.py:110
  83.1 5.3 %convolution_add_fusion.8 = f32[64,1024]{1,0:T(8,128)S(1)} fusion(f32[256]{0:T(256)S(1)} %bitcast.251, f32[256]{0:T(256)S(1)} %bitcast.247, f32[1024]{0:T(1024)S(1)} %bitcast.239, f32[1024]{0:T(1024)S(1)} %bitcast.237, f32[256]{0:T(256)S(1)} %bitcast.249, f32[1024]{0:T(1024)S(1)} %mul.9761, f32[256]{0:T(256)S(1)} %bitcast.245, f32[1024]{0:T(1024)S(1)} %mul.9762, ...), kind=kOutput, calls=%fused_computation.6.clone.1 | convolution fusion | flops 205668352 | bytes 561153 | tf_op jit(solution)/shard_map/while/body/eval_jaxpr/dot_general | solution.py:107
  89.4 1.5 add_multiply_fusion.17
  91.1 5.3 %convolution_add_fusion.9 = f32[64,1024]{1,0:T(8,128)S(1)} fusion(f32[256]{0:T(256)S(1)} %bitcast.250, f32[256]{0:T(256)S(1)} %bitcast.246, f32[1024]{0:T(1024)S(1)} %bitcast.238, f32[1024]{0:T(1024)S(1)} %bitcast.236, f32[256]{0:T(256)S(1)} %bitcast.248, f32[1024]{0:T(1024)S(1)} %mul.9761, f32[256]{0:T(256)S(1)} %bitcast.244, f32[1024]{0:T(1024)S(1)} %mul.9762, ...), kind=kOutput, calls=%fused_computation.5.clone.1 | convolution fusion | flops 205668352 | bytes 561153 | tf_op jit(solution)/shard_map/while/body/eval_jaxpr/dot_general | solution.py:110
  96.4 5.3 %convolution_add_fusion.8 = f32[64,1024]{1,0:T(8,128)S(1)} fusion(f32[256]{0:T(256)S(1)} %bitcast.251, f32[256]{0:T(256)S(1)} %bitcast.247, f32[1024]{0:T(1024)S(1)} %bitcast.239, f32[1024]{0:T(1024)S(1)} %bitcast.237, f32[256]{0:T(256)S(1)} %bitcast.249, f32[1024]{0:T(1024)S(1)} %mul.9761, f32[256]{0:T(256)S(1)} %bitcast.245, f32[1024]{0:T(1024)S(1)} %mul.9762, ...), kind=kOutput, calls=%fused_computation.6.clone.1 | convolution fusion | flops 205668352 | bytes 561153 | tf_op jit(solution)/shard_map/while/body/eval_jaxpr/dot_general | solution.py:107
  102.8 1.5 add_multiply_fusion.17
  104.5 5.3 %convolution_add_fusion.9 = f32[64,1024]{1,0:T(8,128)S(1)} fusion(f32[256]{0:T(256)S(1)} %bitcast.250, f32[256]{0:T(256)S(1)} %bitcast.246, f32[1024]{0:T(1024)S(1)} %bitcast.238, f32[1024]{0:T(1024)S(1)} %bitcast.236, f32[256]{0:T(256)S(1)} %bitcast.248, f32[1024]{0:T(1024)S(1)} %mul.9761, f32[256]{0:T(256)S(1)} %bitcast.244, f32[1024]{0:T(1024)S(1)} %mul.9762, ...), kind=kOutput, calls=%fused_computation.5.clone.1 | convolution fusion | flops 205668352 | bytes 561153 | tf_op jit(solution)/shard_map/while/body/eval_jaxpr/dot_general | solution.py:110
  109.8 5.3 %convolution_add_fusion.8 = f32[64,1024]{1,0:T(8,128)S(1)} fusion(f32[256]{0:T(256)S(1)} %bitcast.251, f32[256]{0:T(256)S(1)} %bitcast.247, f32[1024]{0:T(1024)S(1)} %bitcast.239, f32[1024]{0:T(1024)S(1)} %bitcast.237, f32[256]{0:T(256)S(1)} %bitcast.249, f32[1024]{0:T(1024)S(1)} %mul.9761, f32[256]{0:T(256)S(1)} %bitcast.245, f32[1024]{0:T(1024)S(1)} %mul.9762, ...), kind=kOutput, calls=%fused_computation.6.clone.1 | convolution fusion | flops 205668352 | bytes 561153 | tf_op jit(solution)/shard_map/while/body/eval_jaxpr/dot_general | solution.py:107
  116.1 1.5 add_multiply_fusion.17
  117.8 5.3 %convolution_add_fusion.9 = f32[64,1024]{1,0:T(8,128)S(1)} fusion(f32[256]{0:T(256)S(1)} %bitcast.250, f32[256]{0:T(256)S(1)} %bitcast.246, f32[1024]{0:T(1024)S(1)} %bitcast.238, f32[1024]{0:T(1024)S(1)} %bitcast.236, f32[256]{0:T(256)S(1)} %bitcast.248, f32[1024]{0:T(1024)S(1)} %mul.9761, f32[256]{0:T(256)S(1)} %bitcast.244, f32[1024]{0:T(1024)S(1)} %mul.9762, ...), kind=kOutput, calls=%fused_computation.5.clone.1 | convolution fusion | flops 205668352 | bytes 561153 | tf_op jit(solution)/shard_map/while/body/eval_jaxpr/dot_general | solution.py:110
  123.1 5.3 %convolution_add_fusion.8 = f32[64,1024]{1,0:T(8,128)S(1)} fusion(f32[256]{0:T(256)S(1)} %bitcast.251, f32[256]{0:T(256)S(1)} %bitcast.247, f32[1024]{0:T(1024)S(1)} %bitcast.239, f32[1024]{0:T(1024)S(1)} %bitcast.237, f32[256]{0:T(256)S(1)} %bitcast.249, f32[1024]{0:T(1024)S(1)} %mul.9761, f32[256]{0:T(256)S(1)} %bitcast.245, f32[1024]{0:T(1024)S(1)} %mul.9762, ...), kind=kOutput, calls=%fused_computation.6.clone.1 | convolution fusion | flops 205668352 | bytes 561153 | tf_op jit(solution)/shard_map/while/body/eval_jaxpr/dot_general | solution.py:107
  129.4 1.5 add_multiply_fusion.17
  131.1 5.3 %convolution_add_fusion.9 = f32[64,1024]{1,0:T(8,128)S(1)} fusion(f32[256]{0:T(256)S(1)} %bitcast.250, f32[256]{0:T(256)S(1)} %bitcast.246, f32[1024]{0:T(1024)S(1)} %bitcast.238, f32[1024]{0:T(1024)S(1)} %bitcast.236, f32[256]{0:T(256)S(1)} %bitcast.248, f32[1024]{0:T(1024)S(1)} %mul.9761, f32[256]{0:T(256)S(1)} %bitcast.244, f32[1024]{0:T(1024)S(1)} %mul.9762, ...), kind=kOutput, calls=%fused_computation.5.clone.1 | convolution fusion | flops 205668352 | bytes 561153 | tf_op jit(solution)/shard_map/while/body/eval_jaxpr/dot_general | solution.py:110
  136.4 5.3 %convolution_add_fusion.8 = f32[64,1024]{1,0:T(8,128)S(1)} fusion(f32[256]{0:T(256)S(1)} %bitcast.251, f32[256]{0:T(256)S(1)} %bitcast.247, f32[1024]{0:T(1024)S(1)} %bitcast.239, f32[1024]{0:T(1024)S(1)} %bitcast.237, f32[256]{0:T(256)S(1)} %bitcast.249, f32[1024]{0:T(1024)S(1)} %mul.9761, f32[256]{0:T(256)S(1)} %bitcast.245, f32[1024]{0:T(1024)S(1)} %mul.9762, ...), kind=kOutput, calls=%fused_computation.6.clone.1 | convolution fusion | flops 205668352 | bytes 561153 | tf_op jit(solution)/shard_map/while/body/eval_jaxpr/dot_general | solution.py:107
  142.8 1.5 add_multiply_fusion.17
  144.5 5.3 %convolution_add_fusion.9 = f32[64,1024]{1,0:T(8,128)S(1)} fusion(f32[256]{0:T(256)S(1)} %bitcast.250, f32[256]{0:T(256)S(1)} %bitcast.246, f32[1024]{0:T(1024)S(1)} %bitcast.238, f32[1024]{0:T(1024)S(1)} %bitcast.236, f32[256]{0:T(256)S(1)} %bitcast.248, f32[1024]{0:T(1024)S(1)} %mul.9761, f32[256]{0:T(256)S(1)} %bitcast.244, f32[1024]{0:T(1024)S(1)} %mul.9762, ...), kind=kOutput, calls=%fused_computation.5.clone.1 | convolution fusion | flops 205668352 | bytes 561153 | tf_op jit(solution)/shard_map/while/body/eval_jaxpr/dot_general | solution.py:110
  149.8 5.3 %convolution_add_fusion.8 = f32[64,1024]{1,0:T(8,128)S(1)} fusion(f32[256]{0:T(256)S(1)} %bitcast.251, f32[256]{0:T(256)S(1)} %bitcast.247, f32[1024]{0:T(1024)S(1)} %bitcast.239, f32[1024]{0:T(1024)S(1)} %bitcast.237, f32[256]{0:T(256)S(1)} %bitcast.249, f32[1024]{0:T(1024)S(1)} %mul.9761, f32[256]{0:T(256)S(1)} %bitcast.245, f32[1024]{0:T(1024)S(1)} %mul.9762, ...), kind=kOutput, calls=%fused_computation.6.clone.1 | convolution fusion | flops 205668352 | bytes 561153 | tf_op jit(solution)/shard_map/while/body/eval_jaxpr/dot_general | solution.py:107
  156.1 1.5 add_multiply_fusion.17
  157.8 5.3 %convolution_add_fusion.9 = f32[64,1024]{1,0:T(8,128)S(1)} fusion(f32[256]{0:T(256)S(1)} %bitcast.250, f32[256]{0:T(256)S(1)} %bitcast.246, f32[1024]{0:T(1024)S(1)} %bitcast.238, f32[1024]{0:T(1024)S(1)} %bitcast.236, f32[256]{0:T(256)S(1)} %bitcast.248, f32[1024]{0:T(1024)S(1)} %mul.9761, f32[256]{0:T(256)S(1)} %bitcast.244, f32[1024]{0:T(1024)S(1)} %mul.9762, ...), kind=kOutput, calls=%fused_computation.5.clone.1 | convolution fusion | flops 205668352 | bytes 561153 | tf_op jit(solution)/shard_map/while/body/eval_jaxpr/dot_general | solution.py:110
  163.1 5.3 %convolution_add_fusion.8 = f32[64,1024]{1,0:T(8,128)S(1)} fusion(f32[256]{0:T(256)S(1)} %bitcast.251, f32[256]{0:T(256)S(1)} %bitcast.247, f32[1024]{0:T(1024)S(1)} %bitcast.239, f32[1024]{0:T(1024)S(1)} %bitcast.237, f32[256]{0:T(256)S(1)} %bitcast.249, f32[1024]{0:T(1024)S(1)} %mul.9761, f32[256]{0:T(256)S(1)} %bitcast.245, f32[1024]{0:T(1024)S(1)} %mul.9762, ...), kind=kOutput, calls=%fused_computation.6.clone.1 | convolution fusion | flops 205668352 | bytes 561153 | tf_op jit(solution)/shard_map/while/body/eval_jaxpr/dot_general | solution.py:107
  169.5 1.5 add_multiply_fusion.17
  171.1 5.3 %convolution_add_fusion.9 = f32[64,1024]{1,0:T(8,128)S(1)} fusion(f32[256]{0:T(256)S(1)} %bitcast.250, f32[256]{0:T(256)S(1)} %bitcast.246, f32[1024]{0:T(1024)S(1)} %bitcast.238, f32[1024]{0:T(1024)S(1)} %bitcast.236, f32[256]{0:T(256)S(1)} %bitcast.248, f32[1024]{0:T(1024)S(1)} %mul.9761, f32[256]{0:T(256)S(1)} %bitcast.244, f32[1024]{0:T(1024)S(1)} %mul.9762, ...), kind=kOutput, calls=%fused_computation.5.clone.1 | convolution fusion | flops 205668352 | bytes 561153 | tf_op jit(solution)/shard_map/while/body/eval_jaxpr/dot_general | solution.py:110
  176.4 5.3 %convolution_add_fusion.8 = f32[64,1024]{1,0:T(8,128)S(1)} fusion(f32[256]{0:T(256)S(1)} %bitcast.251, f32[256]{0:T(256)S(1)} %bitcast.247, f32[1024]{0:T(1024)S(1)} %bitcast.239, f32[1024]{0:T(1024)S(1)} %bitcast.237, f32[256]{0:T(256)S(1)} %bitcast.249, f32[1024]{0:T(1024)S(1)} %mul.9761, f32[256]{0:T(256)S(1)} %bitcast.245, f32[1024]{0:T(1024)S(1)} %mul.9762, ...), kind=kOutput, calls=%fused_computation.6.clone.1 | convolution fusion | flops 205668352 | bytes 561153 | tf_op jit(solution)/shard_map/while/body/eval_jaxpr/dot_general | solution.py:107
  182.8 1.5 add_multiply_fusion.17
  184.5 5.3 %convolution_add_fusion.9 = f32[64,1024]{1,0:T(8,128)S(1)} fusion(f32[256]{0:T(256)S(1)} %bitcast.250, f32[256]{0:T(256)S(1)} %bitcast.246, f32[1024]{0:T(1024)S(1)} %bitcast.238, f32[1024]{0:T(1024)S(1)} %bitcast.236, f32[256]{0:T(256)S(1)} %bitcast.248, f32[1024]{0:T(1024)S(1)} %mul.9761, f32[256]{0:T(256)S(1)} %bitcast.244, f32[1024]{0:T(1024)S(1)} %mul.9762, ...), kind=kOutput, calls=%fused_computation.5.clone.1 | convolution fusion | flops 205668352 | bytes 561153 | tf_op jit(solution)/shard_map/while/body/eval_jaxpr/dot_general | solution.py:110
  189.8 5.3 %convolution_add_fusion.8 = f32[64,1024]{1,0:T(8,128)S(1)} fusion(f32[256]{0:T(256)S(1)} %bitcast.251, f32[256]{0:T(256)S(1)} %bitcast.247, f32[1024]{0:T(1024)S(1)} %bitcast.239, f32[1024]{0:T(1024)S(1)} %bitcast.237, f32[256]{0:T(256)S(1)} %bitcast.249, f32[1024]{0:T(1024)S(1)} %mul.9761, f32[256]{0:T(256)S(1)} %bitcast.245, f32[1024]{0:T(1024)S(1)} %mul.9762, ...), kind=kOutput, calls=%fused_computation.6.clone.1 | convolution fusion | flops 205668352 | bytes 561153 | tf_op jit(solution)/shard_map/while/body/eval_jaxpr/dot_general | solution.py:107
  196.1 1.5 add_multiply_fusion.17
  197.8 5.3 %convolution_add_fusion.9 = f32[64,1024]{1,0:T(8,128)S(1)} fusion(f32[256]{0:T(256)S(1)} %bitcast.250, f32[256]{0:T(256)S(1)} %bitcast.246, f32[1024]{0:T(1024)S(1)} %bitcast.238, f32[1024]{0:T(1024)S(1)} %bitcast.236, f32[256]{0:T(256)S(1)} %bitcast.248, f32[1024]{0:T(1024)S(1)} %mul.9761, f32[256]{0:T(256)S(1)} %bitcast.244, f32[1024]{0:T(1024)S(1)} %mul.9762, ...), kind=kOutput, calls=%fused_computation.5.clone.1 | convolution fusion | flops 205668352 | bytes 561153 | tf_op jit(solution)/shard_map/while/body/eval_jaxpr/dot_general | solution.py:110
  203.1 5.3 %convolution_add_fusion.8 = f32[64,1024]{1,0:T(8,128)S(1)} fusion(f32[256]{0:T(256)S(1)} %bitcast.251, f32[256]{0:T(256)S(1)} %bitcast.247, f32[1024]{0:T(1024)S(1)} %bitcast.239, f32[1024]{0:T(1024)S(1)} %bitcast.237, f32[256]{0:T(256)S(1)} %bitcast.249, f32[1024]{0:T(1024)S(1)} %mul.9761, f32[256]{0:T(256)S(1)} %bitcast.245, f32[1024]{0:T(1024)S(1)} %mul.9762, ...), kind=kOutput, calls=%fused_computation.6.clone.1 | convolution fusion | flops 205668352 | bytes 561153 | tf_op jit(solution)/shard_map/while/body/eval_jaxpr/dot_general | solution.py:107
  209.5 1.5 add_multiply_fusion.17
  211.2 5.3 %convolution_add_fusion.9 = f32[64,1024]{1,0:T(8,128)S(1)} fusion(f32[256]{0:T(256)S(1)} %bitcast.250, f32[256]{0:T(256)S(1)} %bitcast.246, f32[1024]{0:T(1024)S(1)} %bitcast.238, f32[1024]{0:T(1024)S(1)} %bitcast.236, f32[256]{0:T(256)S(1)} %bitcast.248, f32[1024]{0:T(1024)S(1)} %mul.9761, f32[256]{0:T(256)S(1)} %bitcast.244, f32[1024]{0:T(1024)S(1)} %mul.9762, ...), kind=kOutput, calls=%fused_computation.5.clone.1 | convolution fusion | flops 205668352 | bytes 561153 | tf_op jit(solution)/shard_map/while/body/eval_jaxpr/dot_general | solution.py:110
  216.5 5.3 %convolution_add_fusion.8 = f32[64,1024]{1,0:T(8,128)S(1)} fusion(f32[256]{0:T(256)S(1)} %bitcast.251, f32[256]{0:T(256)S(1)} %bitcast.247, f32[1024]{0:T(1024)S(1)} %bitcast.239, f32[1024]{0:T(1024)S(1)} %bitcast.237, f32[256]{0:T(256)S(1)} %bitcast.249, f32[1024]{0:T(1024)S(1)} %mul.9761, f32[256]{0:T(256)S(1)} %bitcast.245, f32[1024]{0:T(1024)S(1)} %mul.9762, ...), kind=kOutput, calls=%fused_computation.6.clone.1 | convolution fusion | flops 205668352 | bytes 561153 | tf_op jit(solution)/shard_map/while/body/eval_jaxpr/dot_general | solution.py:107
  222.8 1.5 add_multiply_fusion.17
  224.5 5.3 %convolution_add_fusion.9 = f32[64,1024]{1,0:T(8,128)S(1)} fusion(f32[256]{0:T(256)S(1)} %bitcast.250, f32[256]{0:T(256)S(1)} %bitcast.246, f32[1024]{0:T(1024)S(1)} %bitcast.238, f32[1024]{0:T(1024)S(1)} %bitcast.236, f32[256]{0:T(256)S(1)} %bitcast.248, f32[1024]{0:T(1024)S(1)} %mul.9761, f32[256]{0:T(256)S(1)} %bitcast.244, f32[1024]{0:T(1024)S(1)} %mul.9762, ...), kind=kOutput, calls=%fused_computation.5.clone.1 | convolution fusion | flops 205668352 | bytes 561153 | tf_op jit(solution)/shard_map/while/body/eval_jaxpr/dot_general | solution.py:110
  229.8 5.3 %convolution_add_fusion.8 = f32[64,1024]{1,0:T(8,128)S(1)} fusion(f32[256]{0:T(256)S(1)} %bitcast.251, f32[256]{0:T(256)S(1)} %bitcast.247, f32[1024]{0:T(1024)S(1)} %bitcast.239, f32[1024]{0:T(1024)S(1)} %bitcast.237, f32[256]{0:T(256)S(1)} %bitcast.249, f32[1024]{0:T(1024)S(1)} %mul.9761, f32[256]{0:T(256)S(1)} %bitcast.245, f32[1024]{0:T(1024)S(1)} %mul.9762, ...), kind=kOutput, calls=%fused_computation.6.clone.1 | convolution fusion | flops 205668352 | bytes 561153 | tf_op jit(solution)/shard_map/while/body/eval_jaxpr/dot_general | solution.py:107
  236.2 1.5 add_multiply_fusion.17
  237.8 5.3 %convolution_add_fusion.9 = f32[64,1024]{1,0:T(8,128)S(1)} fusion(f32[256]{0:T(256)S(1)} %bitcast.250, f32[256]{0:T(256)S(1)} %bitcast.246, f32[1024]{0:T(1024)S(1)} %bitcast.238, f32[1024]{0:T(1024)S(1)} %bitcast.236, f32[256]{0:T(256)S(1)} %bitcast.248, f32[1024]{0:T(1024)S(1)} %mul.9761, f32[256]{0:T(256)S(1)} %bitcast.244, f32[1024]{0:T(1024)S(1)} %mul.9762, ...), kind=kOutput, calls=%fused_computation.5.clone.1 | convolution fusion | flops 205668352 | bytes 561153 | tf_op jit(solution)/shard_map/while/body/eval_jaxpr/dot_general | solution.py:110
  243.1 5.3 %convolution_add_fusion.8 = f32[64,1024]{1,0:T(8,128)S(1)} fusion(f32[256]{0:T(256)S(1)} %bitcast.251, f32[256]{0:T(256)S(1)} %bitcast.247, f32[1024]{0:T(1024)S(1)} %bitcast.239, f32[1024]{0:T(1024)S(1)} %bitcast.237, f32[256]{0:T(256)S(1)} %bitcast.249, f32[1024]{0:T(1024)S(1)} %mul.9761, f32[256]{0:T(256)S(1)} %bitcast.245, f32[1024]{0:T(1024)S(1)} %mul.9762, ...), kind=kOutput, calls=%fused_computation.6.clone.1 | convolution fusion | flops 205668352 | bytes 561153 | tf_op jit(solution)/shard_map/while/body/eval_jaxpr/dot_general | solution.py:107
  252.1 2.4 subtract_bitcast_fusion.6
  256.4 1.3 fusion.112
  258.9 12.9 %collective-permute-done.1 = f32[2,64,1024]{2,1,0:T(8,128)S(1)} collective-permute-done((f32[2,64,1024]{2,1,0:T(8,128)S(1)}, f32[2,64,1024]{2,1,0:T(8,128)S(1)}, u32[]{:S(2)}, u32[]{:S(2)}) %collective-permute-start.1) | collective-permute-done | bytes 524320 | tf_op jit(solution)/shard_map/ppermute | solution.py:15
  271.9 2.4 subtract_bitcast_fusion.4
  278.0 12.0 %collective-permute-done.2 = f32[2,64,1024]{2,1,0:T(8,128)S(1)} collective-permute-done((f32[2,64,1024]{2,1,0:T(8,128)S(1)}, f32[2,64,1024]{2,1,0:T(8,128)S(1)}, u32[]{:S(2)}, u32[]{:S(2)}) %collective-permute-start.2) | collective-permute-done | bytes 524320 | tf_op jit(solution)/shard_map/ppermute | solution.py:15
  290.0 2.7 subtract_bitcast_fusion.2
  294.6 1.3 fusion.110
  296.7 11.5 %collective-permute-done.3 = f32[2,64,1024]{2,1,0:T(8,128)S(1)} collective-permute-done((f32[2,64,1024]{2,1,0:T(8,128)S(1)}, f32[2,64,1024]{2,1,0:T(8,128)S(1)}, u32[]{:S(2)}, u32[]{:S(2)}) %collective-permute-start.3) | collective-permute-done | bytes 524320 | tf_op jit(solution)/shard_map/ppermute | solution.py:15
  308.3 2.4 subtract_bitcast_fusion
  (296 shorter events, 40.8 us)
Async XLA Ops:
  0.0 10.6 %copy-start.1 = (s32[2048,1]{0,1:T(1,128)S(1)}, s32[2048,1]{0,1:T(1,128)}, u32[]{:S(2)}) copy-start(s32[2048,1]{0,1:T(1,128)} %param.27) | copy-start | bytes 24580
  0.0 10.7 %copy-start.4 = (s32[2,2048]{1,0:T(2,128)S(1)}, s32[2,2048]{1,0:T(2,128)}, u32[]{:S(2)}) copy-start(s32[2,2048]{1,0:T(2,128)} %param.28) | copy-start | bytes 49156
  0.0 10.8 %copy-start.5 = (f32[2,2048]{1,0:T(2,128)S(1)}, f32[2,2048]{1,0:T(2,128)}, u32[]{:S(2)}) copy-start(f32[2,2048]{1,0:T(2,128)} %param.29) | copy-start | bytes 49156
  11.2 1.6 copy-start
  11.3 17.3 %copy-start.10 = (s32[4]{0:T(128)S(1)}, s32[4]{0:T(128)}, u32[]{:S(2)}) copy-start(s32[4]{0:T(128)} %param.30) | copy-start | bytes 52
  11.3 19.4 %copy-start.8 = (f32[8]{0:T(128)S(1)}, f32[8]{0:T(128)}, u32[]{:S(2)}) copy-start(f32[8]{0:T(128)} %constant.635) | copy-start | bytes 100
  11.3 19.4 %copy-start.9 = (f32[8]{0:T(128)S(1)}, f32[8]{0:T(128)}, u32[]{:S(2)}) copy-start(f32[8]{0:T(128)} %constant.636) | copy-start | bytes 100
  20.5 14.6 %all-to-all-start = ((f32[32,1,512]{2,1,0:T(1,128)}), f32[32,1,512]{2,1,0:T(1,128)S(1)}, u32[]{:S(2)}, u32[]{:S(2)}) async-start(f32[32,1,512]{2,1,0:T(1,128)} %bitcast.15), calls=%async_computation | async-start | bytes 131072 | tf_op jit(solution)/shard_map/all_to_all | solution.py:243
  248.7 1.9 copy-start.6
  248.7 1.9 copy-start.7
  250.0 2.0 collective-permute-start
  252.0 3.1 copy-start.3
  254.5 1.2 copy-start.2
  257.8 14.0 %collective-permute-start.1 = (f32[2,64,1024]{2,1,0:T(8,128)S(1)}, f32[2,64,1024]{2,1,0:T(8,128)S(1)}, u32[]{:S(2)}, u32[]{:S(2)}) collective-permute-start(f32[2,64,1024]{2,1,0:T(8,128)S(1)} %pad_maximum_fusion.1), channel_id=1, source_target_pairs={{0,1},{1,0},{2,3},{3,2},{4,5},{5,4},{6,7},{7,6},{8,9},{9,8},{10,11... | collective-permute-start | bytes 1572872 | tf_op jit(solution)/shard_map/ppermute | solution.py:15
  276.8 13.2 %collective-permute-start.2 = (f32[2,64,1024]{2,1,0:T(8,128)S(1)}, f32[2,64,1024]{2,1,0:T(8,128)S(1)}, u32[]{:S(2)}, u32[]{:S(2)}) collective-permute-start(f32[2,64,1024]{2,1,0:T(8,128)S(1)} %pad_maximum_fusion.2), channel_id=1, source_target_pairs={{0,16},{8,24},{16,0},{24,8},{1,17},{9,25},{17,1},{25,9},{2,18},{10... | collective-permute-start | bytes 1572872 | tf_op jit(solution)/shard_map/ppermute | solution.py:15
  296.0 12.3 %collective-permute-start.3 = (f32[2,64,1024]{2,1,0:T(8,128)S(1)}, f32[2,64,1024]{2,1,0:T(8,128)S(1)}, u32[]{:S(2)}, u32[]{:S(2)}) collective-permute-start(f32[2,64,1024]{2,1,0:T(8,128)S(1)} %pad_maximum_fusion.3), channel_id=1, source_target_pairs={{0,2},{1,3},{2,0},{3,1},{4,6},{5,7},{6,4},{7,5},{8,10},{9,11},{10,... | collective-permute-start | bytes 1572872 | tf_op jit(solution)/shard_map/ppermute | solution.py:15
where the time goes:
time: 315 us; the launch traced here: 314 us
  matrix products  174 us (55%)
  other arithmetic  56.4 us (18%)
  waiting for transfers between devices  40.5 us (13%)
  local copies, waits for them, and re-layouts  30.6 us (10%)
  starting transfers between devices  9.76 us (3%)
    dot_general x16, matrix products, leaf_terms(): lax.dot_general(basis, imag_part, dims, precision=lax.Precision.HIGHEST,...  84.7 us
    dot_general x16, matrix products, leaf_terms(): lax.dot_general(basis, real_part, dims, precision=lax.Precision.HIGHEST,...  84.6 us
    ppermute x4, waiting for transfers between devices, from_partner(): lax.ppermute(value, axis, [(i, i ^ 1 << distance) for i in range(lax.axis...  37.7 us
    div x17, other arithmetic, phases(): speed_first = (32.0 + scaled[0] + scaled[1] * wave) / 4096.0  24.6 us
    slice x17, local copies, waits for them, and re-layouts, phases(): speed_first = (32.0 + scaled[0] + scaled[1] * wave) / 4096.0  11.1 us
    another operation x4, other arithmetic, merge_box(): jnp.stack([cosine * child[0] - sine * child[1], cosine * child[1] + sine...  9.97 us
    another operation x2, other arithmetic  9.27 us
    all_to_all x1, starting transfers between devices, on_device(): lax.all_to_all(sent, ('bx', 'by'), split_axis=0, concat_axis=0, tiled=True)  7.48 us
  transfers between devices with their start and end apart: 5, of which 5 were waited for; matrix products, arithmetic and copies ran while one was open for 1% of the time, Pallas kernels for 0%

commit v1 on v0

v1 whole, which is shorter than its diff:
```python
import functools

import jax
import jax.numpy as jnp
import numpy as np
from jax import lax
from jax.experimental import pallas as pl
from jax.experimental.pallas import tpu as pltpu
from jax.sharding import PartitionSpec as P

N = 16384
ORDER = 8
NODES = ORDER * ORDER
TGT1 = 32
TGT2 = 32
STEP = 256
UC = 4
CW = UC * TGT2
CHUNKS = TGT1 // UC
HALF = 48
MESH = pl.DeviceIdType.MESH
F32 = jnp.float32
BF16 = jnp.bfloat16
NT = (((1,), (1,)), ((), ()))


def node_table():
    counting = np.arange(ORDER) * 1.0
    return 0.5 - 0.5 * np.cos(np.pi * (2.0 * counting + 1.0) / (2.0 * ORDER))


def child_matrix(side):
    nodes = node_table()
    points = 0.5 * (side + nodes)
    rows_all = []
    for target in range(ORDER):
        factor = np.ones(ORDER)
        for source in range(ORDER):
            if source != target:
                factor = factor * (points - nodes[source]) / (nodes[target] - nodes[source])
        rows_all.append(factor)
    return np.stack(rows_all).astype(np.float32)


def merge_tables():
    eye = np.eye(ORDER, dtype=np.float32)
    first = [np.kron(child_matrix(side), eye) for side in (0, 1)]
    second = [np.kron(eye, child_matrix(side)) for side in (0, 1)]
    return np.stack([np.stack(first), np.stack(second)])


def lagrange_scales():
    nodes = node_table()
    scales = np.ones((ORDER, ORDER))
    for target in range(ORDER):
        for source in range(ORDER):
            if source != target:
                scales[target, source] = 1.0 / (nodes[target] - nodes[source])
    return scales.astype(np.float32)


def sine_coefficients():
    y = 0.25 * np.cos(np.pi * (np.arange(400) + 0.5) / 800)
    target = np.sin(2 * np.pi * y) / y
    fit = np.polynomial.chebyshev.Chebyshev.fit(y * y, target, 5, domain=[0.0, 1.0 / 16.0])
    return [float(c) for c in fit.convert(kind=np.polynomial.Polynomial).coef]


SINE = sine_coefficients()


def quarter_sine(y):
    square = y * y
    value = jnp.full_like(y, SINE[5])
    for c in SINE[4::-1]:
        value = value * square + c
    return value * y


def cos_sin(cycles):
    q = cycles - jnp.round(cycles)
    cosine = quarter_sine(0.25 - jnp.abs(q))
    sine = quarter_sine(jnp.maximum(jnp.minimum(q, 0.5 - q), -0.5 - q))
    return cosine, sine


def split(value):
    high = value.astype(BF16)
    return high, (value - high.astype(F32)).astype(BF16)


def pack_kernel(owners, cap, ids_ref, offset_ref, value_ref, tri_ref, out_ref):
    total = ids_ref.shape[1]
    width = 256
    carry = jnp.zeros((owners, 1), F32)
    packed = jnp.zeros((10 * owners, cap), F32)
    for block in range(total // width):
        lanes = slice(block * width, (block + 1) * width)
        ids = ids_ref[:, lanes]
        hit = ids == lax.broadcasted_iota(jnp.int32, (owners, width), 0)
        onehot = hit.astype(F32)
        before = jnp.dot(onehot.astype(BF16), tri_ref[...], preferred_element_type=F32) + carry
        ranks = jnp.sum(before * onehot, axis=0, keepdims=True)
        carry = carry + jnp.sum(onehot, axis=1, keepdims=True)
        slot = lax.broadcasted_iota(jnp.int32, (cap, width), 0)
        place = (slot == ranks.astype(jnp.int32)).astype(F32).astype(BF16)
        parts = []
        for row in range(2):
            offset = offset_ref[row : row + 1, lanes]
            low = offset & 127
            parts += [(offset - low).astype(F32), low.astype(F32)]
        for row in range(2):
            value = value_ref[row : row + 1, lanes]
            high = value.astype(BF16).astype(F32)
            rest = value - high
            middle = rest.astype(BF16).astype(F32)
            parts += [high, middle, rest - middle]
        lhs = jnp.concatenate([onehot * part for part in parts], axis=0).astype(BF16)
        packed = packed + lax.dot_general(lhs, place, NT, preferred_element_type=F32)
    rows = [packed[i * owners : (i + 1) * owners] for i in range(10)]
    fields = [rows[0] + rows[1], rows[2] + rows[3]]
    fields += [(rows[4] + rows[5]) + rows[6], (rows[7] + rows[8]) + rows[9]]
    for i, field in enumerate(fields):
        out_ref[:, i * cap : (i + 1) * cap] = field


def code_of(index, merged):
    code = index * 0
    for bit in range(merged):
        code = code + (index // 2**bit) % 2 * 2 ** (merged - 1 - bit)
    return code


def flipped(index, level):
    return index + 2**level - 2 * 2**level * ((index // 2**level) % 2)


def main_kernel(
    boxes_x, boxes_y, coef_ref, col_ref, merge_ref, scale_ref, node_ref, out_ref,
    hr_ref, hi_ref, zr_ref, zi_ref, basis_ref, acc_ref, sent_ref, got_ref, send_sem, recv_sem,
):
    ix = lax.axis_index("bx")
    iy = lax.axis_index("by")
    partners = []
    for level in range(2):
        partners.append({"bx": flipped(ix, level), "by": iy})
        partners.append({"bx": ix, "by": flipped(iy, level)})
    barrier = pltpu.get_barrier_semaphore()
    for partner in partners:
        pl.semaphore_signal(barrier, inc=1, device_id=partner, device_id_type=MESH)

    wx = N // boxes_x
    wy = N // boxes_y
    steps = col_ref.shape[0]
    scaled = [coef_ref[i].astype(F32) for i in range(4)]

    def speeds(wave):
        first = (32.0 + scaled[0] + scaled[1] * wave) * (1.0 / 4096.0)
        second = (32.0 + scaled[2] + scaled[3] * wave) * (1.0 / 4096.0)
        return first, second

    row = lax.broadcasted_iota(jnp.int32, (2 * HALF, 1), 0)
    odd = (row >= HALF).astype(jnp.int32)
    m = (2 * (row - HALF * odd) + odd).astype(F32)
    wave = cos_sin(64.0 / N * ((m + 0.5) * boxes_x + 0.5 * boxes_y))[1]
    speed_first, speed_second = speeds(wave)
    sq_first = speed_first * speed_first
    sq_second = speed_second * speed_second
    m_scale = (2.0 * m + 1.0) * (boxes_x / (2.0 * N))
    v_scale = lax.broadcasted_iota(jnp.int32, (TGT2, 1), 0).astype(F32) * (boxes_y / N)
    half_turn = ((ix + iy) % 2).astype(F32) * 0.5
    corner_first = (ix * wx).astype(F32)
    corner_second = (iy * wy).astype(F32)
    node_values = node_table()
    order_row = lax.broadcasted_iota(jnp.int32, (ORDER, 1), 0)

    def lagrange(coords):
        factor = jnp.ones((ORDER, STEP), F32)
        for source in range(ORDER):
            term = (coords - float(node_values[source])) * scale_ref[:, source : source + 1]
            factor = factor * jnp.where(order_row == source, 1.0, term)
        return factor

    def tables(step, carry):
        o1 = col_ref[step, 0:1, :]
        o2 = col_ref[step, 1:2, :]
        re = col_ref[step, 2:3, :]
        im = col_ref[step, 3:4, :]
        k1 = o1 + corner_first
        k2 = o2 + corner_second
        linear = m_scale * o1 + (o2 * (boxes_y / (2.0 * N)) + half_turn)
        root = jnp.sqrt(1.0 + sq_first * (k1 * k1) + sq_second * (k2 * k2))
        cosine, sine = cos_sin((linear - jnp.round(linear)) + root)
        hr_ref[step] = cosine * re - sine * im
        hi_ref[step] = cosine * im + sine * re
        cosine, sine = cos_sin(v_scale * (o2 - o1))
        zr_ref[step] = cosine
        zi_ref[step] = sine
        first = lagrange(o1 * (1.0 / wx))
        second = lagrange(o2 * (1.0 / wy))
        basis = jnp.concatenate([first[t : t + 1] * second for t in range(ORDER)], axis=0)
        high, low = split(basis)
        basis_ref[step] = jnp.concatenate([high, low], axis=0)
        return carry

    lax.fori_loop(0, steps, tables, 0)

    def leaf(chunk):
        def add(step, carry):
            zr = zr_ref[step]
            zi = zi_ref[step]
            reals = []
            imags = []
            for u in range(chunk * UC, (chunk + 1) * UC):
                start = HALF * (u % 2) + u // 2
                hr = hr_ref[step, start : start + TGT2, :]
                hi = hi_ref[step, start : start + TGT2, :]
                reals.append(hr * zr - hi * zi)
                imags.append(hr * zi + hi * zr)
            high, low = split(jnp.concatenate(reals + imags, axis=0))
            basis = basis_ref[step]
            acc_ref[...] += lax.dot_general(
                high, basis, NT, preferred_element_type=F32
            ) + lax.dot_general(low, basis, NT, preferred_element_type=F32)
            return carry

        acc_ref[...] = jnp.zeros_like(acc_ref)
        lax.fori_loop(0, steps, add, 0)
        whole = jnp.transpose(acc_ref[...])
        both = whole[:NODES] + whole[NODES:]
        return both[:, :CW], both[:, CW:]

    lane = lax.broadcasted_iota(jnp.int32, (1, CW), 1)

    def centre(chunk, m1, m2):
        u = (lane // TGT2 + chunk * UC) * 2**m1 + code_of(ix, m1)
        v = lane % TGT2 * 2**m2 + code_of(iy, m2)
        first = (u.astype(F32) + 0.5) * (boxes_x / (N * 2.0**m1))
        second = (v.astype(F32) + 0.5) * (boxes_y / (N * 2.0**m2))
        return first, second

    def roots(place, n1, n2):
        wave = cos_sin(64.0 * (place[0] + place[1]))[1]
        first, second = speeds(wave)
        return jnp.sqrt(1.0 + (first * first) * (n1 * n1) + (second * second) * (n2 * n2))

    def box_nodes(px, py, m1, m2):
        a1 = (px // 2**m1 * (wx * 2**m1)).astype(F32)
        a2 = (py // 2**m2 * (wy * 2**m2)).astype(F32)
        n1 = a1 + float(wx * 2**m1) * node_ref[:, 0:1]
        n2 = a2 + float(wy * 2**m2) * node_ref[:, 1:2]
        return n1, n2

    def merge(chunk, stage, mine, other):
        level, along = stage // 2, stage % 2
        m1, m2 = level + along, level
        new1, new2 = (m1 + 1, m2) if along == 0 else (m1, m2 + 1)
        old_place = centre(chunk, m1, m2)
        new_place = centre(chunk, new1, new2)
        shift1 = (
            (code_of(ix, new1).astype(F32) + 0.5) * (boxes_x / (N * 2.0**new1))
            - (code_of(ix, m1).astype(F32) + 0.5) * (boxes_x / (N * 2.0**m1))
        )
        shift2 = (
            (code_of(iy, new2).astype(F32) + 0.5) * (boxes_y / (N * 2.0**new2))
            - (code_of(iy, m2).astype(F32) + 0.5) * (boxes_y / (N * 2.0**m2))
        )
        px = flipped(ix, level) if along == 0 else ix
        py = flipped(iy, level) if along == 1 else iy
        bit = ((ix if along == 0 else iy) // 2**level) % 2
        lifted = []
        for child, bx, by in ((mine, ix, iy), (other, px, py)):
            n1, n2 = box_nodes(bx, by, m1, m2)
            linear = shift1 * n1 + shift2 * n2
            cycles = (roots(new_place, n1, n2) - roots(old_place, n1, n2)) + linear
            cosine, sine = cos_sin(cycles)
            lifted.append(
                jnp.concatenate(
                    [cosine * child[0] - sine * child[1], cosine * child[1] + sine * child[0]],
                    axis=1,
                )
            )
        low, high = merge_ref[along, 0], merge_ref[along, 1]
        side = bit.astype(F32)
        table_mine = low * (1.0 - side) + high * side
        table_other = low * side + high * (1.0 - side)
        table = jnp.concatenate([table_mine, table_other], axis=1)
        total = jnp.dot(
            table,
            jnp.concatenate(lifted, axis=0),
            precision=lax.Precision.HIGHEST,
            preferred_element_type=F32,
        )
        return total[:, :CW], total[:, CW:]

    def finish(chunk, total):
        place = centre(chunk, 2, 2)
        n1, n2 = box_nodes(ix, iy, 2, 2)
        linear = place[0] * n1 + place[1] * n2
        cosine, sine = cos_sin((linear - jnp.round(linear)) + roots(place, n1, n2))
        lanes = slice(chunk * CW, (chunk + 1) * CW)
        out_ref[0, :, lanes] = cosine * total[0] + sine * total[1]
        out_ref[1, :, lanes] = cosine * total[1] - sine * total[0]

    def exchange(stage, chunk):
        return pltpu.make_async_remote_copy(
            src_ref=sent_ref.at[stage, chunk],
            dst_ref=got_ref.at[stage, chunk],
            send_sem=send_sem.at[stage, chunk],
            recv_sem=recv_sem.at[stage, chunk],
            device_id=partners[stage],
            device_id_type=MESH,
        )

    def send(stage, chunk, value):
        sent_ref[stage, chunk, 0] = value[0]
        sent_ref[stage, chunk, 1] = value[1]
        exchange(stage, chunk).start()

    greeted = False
    for slot in range(CHUNKS + 4):
        if slot < CHUNKS:
            value = leaf(slot)
            if not greeted:
                pl.semaphore_wait(barrier, 4)
                greeted = True
            send(0, slot, value)
        for stage in range(3, -1, -1):
            chunk = slot - 1 - stage
            if 0 <= chunk < CHUNKS:
                exchange(stage, chunk).wait()
                value = merge(chunk, stage, sent_ref.at[stage, chunk], got_ref.at[stage, chunk])
                if stage < 3:
                    send(stage + 1, chunk, value)
                else:
                    finish(chunk, value)


def on_device(point_box, point_offset, point_value, coef):
    boxes_x = lax.axis_size("bx")
    boxes_y = lax.axis_size("by")
    assert boxes_y == 2 * boxes_x
    owners = boxes_x * boxes_y
    held = point_box.shape[0]
    cap = 2 * held // owners
    vmem = pl.BlockSpec(memory_space=pltpu.VMEM)
    tri = jnp.asarray(np.triu(np.ones((256, 256), np.float32), 1), BF16)
    sent = pl.pallas_call(
        functools.partial(pack_kernel, owners, cap),
        out_shape=jax.ShapeDtypeStruct((owners, 4 * cap), F32),
        in_specs=[vmem] * 4,
        out_specs=vmem,
        compiler_params=pltpu.CompilerParams(vmem_limit_bytes=16 << 20),
        name="pack",
    )(point_box.reshape(1, held), point_offset, point_value, tri)
    arrived = lax.all_to_all(sent, ("bx", "by"), split_axis=0, concat_axis=0, tiled=True)
    slots = owners * cap
    steps = slots // STEP
    columns = arrived.reshape(owners, 4, cap).transpose(1, 0, 2).reshape(4, steps, STEP)
    columns = columns.transpose(1, 0, 2)
    nodes = node_table().astype(np.float32)
    node_pairs = np.stack([np.repeat(nodes, ORDER), np.tile(nodes, ORDER)], axis=1)
    return pl.pallas_call(
        functools.partial(main_kernel, boxes_x, boxes_y),
        out_shape=jax.ShapeDtypeStruct((2, NODES, TGT1 * TGT2), F32),
        in_specs=[pl.BlockSpec(memory_space=pltpu.SMEM)] + [vmem] * 4,
        out_specs=vmem,
        scratch_shapes=[
            pltpu.VMEM((steps, 2 * HALF, STEP), F32),
            pltpu.VMEM((steps, 2 * HALF, STEP), F32),
            pltpu.VMEM((steps, TGT2, STEP), F32),
            pltpu.VMEM((steps, TGT2, STEP), F32),
            pltpu.VMEM((steps, 2 * NODES, STEP), BF16),
            pltpu.VMEM((2 * CW, 2 * NODES), F32),
            pltpu.VMEM((4, CHUNKS, 2, NODES, CW), F32),
            pltpu.VMEM((4, CHUNKS, 2, NODES, CW), F32),
            pltpu.SemaphoreType.DMA((4, CHUNKS)),
            pltpu.SemaphoreType.DMA((4, CHUNKS)),
        ],
        compiler_params=pltpu.CompilerParams(
            collective_id=0, has_side_effects=True, vmem_limit_bytes=40 << 20
        ),
        name="butterfly",
    )(coef, columns, jnp.asarray(merge_tables()), jnp.asarray(lagrange_scales()), jnp.asarray(node_pairs))


def solution(mesh):
    in_specs = (P(("bx", "by"), None), P(None, ("bx", "by")), P(None, ("bx", "by")), P())
    out_specs = P(None, None, ("bx", "by"))
    return jax.shard_map(
        on_device, mesh=mesh, in_specs=in_specs, out_specs=out_specs, check_vma=False
    )
```

time: 315 us -> 83.9 us (0.27)
  matrix products: 174 us -> 0 us
  Pallas kernels: 0 us -> 64.4 us
  other arithmetic: 56.4 us -> 0 us
  waiting for transfers between devices: 40.5 us -> 0 us
  local copies, waits for them, and re-layouts: 30.6 us -> 4.57 us
  blocking collectives: 0 us -> 14.4 us
  starting transfers between devices: 9.76 us -> 0 us
    dot_general x40 -> x0, matrix products: 174 us -> none  [the longest x16 84.7 us: leaf_terms(): lax.dot_general(basis, imag_part, dims, precision=lax.Precision.HIGHEST,...]
    pallas_call x0 -> x2, Pallas kernels: none -> 64.4 us  [the longest x1 63.1 us: on_device(): pl.pallas_call(functools.partial(main_kernel, boxes_x, boxes_y), out_shap...]
    ppermute x4 -> x0, waiting for transfers between devices: 37.7 us -> none  [from_partner(): lax.ppermute(value, axis, [(i, i ^ 1 << distance) for i in range(lax.axis...]
    div x17 -> x0, other arithmetic: 24.6 us -> none  [phases(): speed_first = (32.0 + scaled[0] + scaled[1] * wave) / 4096.0]
    another operation x13 -> x0, other arithmetic: 21.5 us -> none  [the longest x4 9.97 us: merge_box(): jnp.stack([cosine * child[0] - sine * child[1], cosine * child[1] + sine...]
    all_to_all x0 -> x1, blocking collectives: none -> 14.4 us  [on_device(): lax.all_to_all(sent, ('bx', 'by'), split_axis=0, concat_axis=0, tiled=True)]
    slice x19 -> x0, local copies, waits for them, and re-layouts: 11.2 us -> none  [the longest x17 11.1 us: phases(): speed_first = (32.0 + scaled[0] + scaled[1] * wave) / 4096.0]
    all_to_all x1 -> x0, starting transfers between devices: 7.48 us -> none  [on_device(): lax.all_to_all(sent, ('bx', 'by'), split_axis=0, concat_axis=0, tiled=True)]
  transfers between devices with their start and end apart: 5 -> 0, of which waited for: 5 -> 0; matrix products, arithmetic and copies ran while one was open for 1% -> 0% of each run, Pallas kernels for 0% -> 0%
where the time goes in v1:
time: 83.9 us; the launch traced here: 83.4 us
  Pallas kernels  64.4 us (77%)
  blocking collectives  14.4 us (17%)
  local copies, waits for them, and re-layouts  4.57 us (5%)
    pallas_call x1, Pallas kernels, on_device(): pl.pallas_call(functools.partial(main_kernel, boxes_x, boxes_y), out_shap...  63.1 us
    all_to_all x1, blocking collectives, on_device(): lax.all_to_all(sent, ('bx', 'by'), split_axis=0, concat_axis=0, tiled=True)  14.4 us
    unnamed x17, local copies, waits for them, and re-layouts  4.49 us

profile of v1, /device:TPU:0, one launch (start us, length us, event | category | flops | bytes accessed | tf_op | source)
XLA Modules:
  0.0 83.4 jit_solution(12686612696833450443)
XLA Ops:
  0.0 0.0 copy-start
  0.0 0.9 %copy-done = bf16[256,256]{1,0:T(8,128)(2,1)S(1)} copy-done((bf16[256,256]{1,0:T(8,128)(2,1)S(1)}, bf16[256,256]{1,0:T(8,128)(2,1)}, u32[]{:S(2)}) %copy-start) | copy-done | bytes 131096
  0.9 0.0 copy-start.3
  0.9 0.7 copy-done.3
  1.6 0.0 copy-start.4
  1.6 0.7 copy-done.4
  2.3 0.0 copy-start.5
  2.3 0.7 copy-done.5
  3.0 1.3 %pack.1 = f32[32,512]{1,0:T(8,128)S(1)} custom-call(s32[1,2048]{1,0:T(1,128)S(1)} %bitcast.11, s32[2,2048]{1,0:T(2,128)S(1)} %copy-done.3, f32[2,2048]{1,0:T(2,128)S(1)} %copy-done.4, bf16[256,256]{1,0:T(8,128)(2,1)S(1)} %copy-done), custom_call_target="tpu_custom_call" | custom-call | tf_op jit(solution)/shard_map/pack/pallas_call | solution.py:348
  4.4 0.0 copy-start.1
  4.4 0.1 copy.9
  4.5 0.0 copy-start.2
  4.5 0.0 copy-start.6
  4.5 14.4 %all_to_all.9 = f32[32,1,512]{2,1,0:T(1,128)S(1)} all-to-all(f32[32,1,512]{2,1,0:T(1,128)S(1)} %copy.9), channel_id=1, replica_groups=mesh['bx'=4,'by'=8] {'bx','by'}, dimensions={0} | all-to-all | bytes 131072 | tf_op jit(solution)/shard_map/all_to_all | solution.py:356
  18.9 0.0 copy-start.7
  18.9 0.0 copy-done.1
  18.9 0.0 copy-done.2
  18.9 0.0 copy-done.6
  18.9 0.6 copy-done.7
  19.5 63.1 %butterfly.1 = f32[2,64,1024]{2,1,0:T(8,128)S(1)} custom-call(s32[4]{0:T(128)S(1)} %copy-done.7, f32[16,4,256]{2,1,0:T(4,128)S(1)} %bitcast.10, f32[2,2,64,64]{3,2,1,0:T(8,128)S(1)} %copy-done.1, f32[8,8]{1,0:T(8,128)S(1)} %copy-done.6, f32[64,2]{1,0:T(8,128)S(1)} %copy-done.2), custom_call_target="tpu_custom_call" | custom-call | tf_op jit(solution)/shard_map/butterfly/pallas_call | solution.py:363
  82.6 0.8 copy.11
Async XLA Ops:
  0.0 0.9 %copy-start = (bf16[256,256]{1,0:T(8,128)(2,1)S(1)}, bf16[256,256]{1,0:T(8,128)(2,1)}, u32[]{:S(2)}) copy-start(bf16[256,256]{1,0:T(8,128)(2,1)} %constant.8.clone.tri_ref) | copy-start | bytes 393220
  0.9 0.7 copy-start.3
  1.6 0.7 copy-start.4
  2.3 0.7 copy-start.5
  4.4 14.5 %copy-start.1 = (f32[2,2,64,64]{3,2,1,0:T(8,128)S(1)}, f32[2,2,64,64]{3,2,1,0:T(8,128)}, u32[]{:S(2)}) copy-start(f32[2,2,64,64]{3,2,1,0:T(8,128)} %constant.9.clone.merge_ref) | copy-start | bytes 196612
  4.5 14.4 %copy-start.2 = (f32[64,2]{1,0:T(8,128)S(1)}, f32[64,2]{1,0:T(8,128)}, u32[]{:S(2)}) copy-start(f32[64,2]{1,0:T(8,128)} %constant.11.clone.node_ref) | copy-start | bytes 1540
  4.5 14.4 %copy-start.6 = (f32[8,8]{1,0:T(8,128)S(1)}, f32[8,8]{1,0:T(8,128)}, u32[]{:S(2)}) copy-start(f32[8,8]{1,0:T(8,128)} %constant.10.clone.scale_ref) | copy-start | bytes 772
  18.9 0.7 copy-start.7

commit v2 on v1

--- a/solution.py
+++ b/solution.py
@@ -17,6 +17,10 @@
 UC = 4
 CW = UC * TGT2
 CHUNKS = TGT1 // UC
+GROUP = 2
+GU = GROUP * UC
+GW = GROUP * CW
+UNROLL = 2
 HALF = 48
 MESH = pl.DeviceIdType.MESH
 F32 = jnp.float32
@@ -89,7 +93,23 @@
     return high, (value - high.astype(F32)).astype(BF16)
 
 
-def pack_kernel(owners, cap, ids_ref, offset_ref, value_ref, tri_ref, out_ref):
+def pack_kernel(
+    boxes_y, owners, cap, ids_ref, offset_ref, value_ref, tri_ref, out_ref,
+    sent_ref, got_ref, send_sem, recv_sem,
+):
+    me = lax.axis_index("bx") * boxes_y + lax.axis_index("by")
+    barrier = pltpu.get_barrier_semaphore()
+
+    def place_of(distance):
+        target = (me + distance) % owners
+        return target, {"bx": target // boxes_y, "by": target % boxes_y}
+
+    def greet(distance, carry):
+        where = place_of(distance)[1]
+        pl.semaphore_signal(barrier, inc=1, device_id=where, device_id_type=MESH)
+        return carry
+
+    lax.fori_loop(1, owners, greet, 0)
     total = ids_ref.shape[1]
     width = 256
     carry = jnp.zeros((owners, 1), F32)
@@ -120,8 +140,34 @@
     rows = [packed[i * owners : (i + 1) * owners] for i in range(10)]
     fields = [rows[0] + rows[1], rows[2] + rows[3]]
     fields += [(rows[4] + rows[5]) + rows[6], (rows[7] + rows[8]) + rows[9]]
-    for i, field in enumerate(fields):
-        out_ref[:, i * cap : (i + 1) * cap] = field
+    joined = jnp.concatenate(fields, axis=1)
+    for i in range(4 * cap // 128):
+        sent_ref[:, i, :] = joined[:, i * 128 : (i + 1) * 128]
+
+    def copy(distance):
+        target, where = place_of(distance)
+        return pltpu.make_async_remote_copy(
+            src_ref=sent_ref.at[target],
+            dst_ref=got_ref.at[me],
+            send_sem=send_sem.at[distance],
+            recv_sem=recv_sem.at[distance],
+            device_id=where,
+            device_id_type=MESH,
+        )
+
+    def begin(distance, carry):
+        copy(distance).start()
+        return carry
+
+    def end(distance, carry):
+        copy(distance).wait()
+        return carry
+
+    pl.semaphore_wait(barrier, owners - 1)
+    lax.fori_loop(1, owners, begin, 0)
+    got_ref[me] = sent_ref[me]
+    lax.fori_loop(1, owners, end, 0)
+    out_ref[...] = got_ref[...]
 
 
 def code_of(index, merged):
@@ -200,35 +246,42 @@
         second = lagrange(o2 * (1.0 / wy))
         basis = jnp.concatenate([first[t : t + 1] * second for t in range(ORDER)], axis=0)
         high, low = split(basis)
-        basis_ref[step] = jnp.concatenate([high, low], axis=0)
+        both = jnp.concatenate([high.astype(F32), low.astype(F32)], axis=0)
+        basis_ref[step] = jnp.transpose(both).astype(BF16)
         return carry
 
     lax.fori_loop(0, steps, tables, 0)
 
-    def leaf(chunk):
-        def add(step, carry):
-            zr = zr_ref[step]
-            zi = zi_ref[step]
-            reals = []
-            imags = []
-            for u in range(chunk * UC, (chunk + 1) * UC):
-                start = HALF * (u % 2) + u // 2
-                hr = hr_ref[step, start : start + TGT2, :]
-                hi = hi_ref[step, start : start + TGT2, :]
-                reals.append(hr * zr - hi * zi)
-                imags.append(hr * zi + hi * zr)
-            high, low = split(jnp.concatenate(reals + imags, axis=0))
-            basis = basis_ref[step]
-            acc_ref[...] += lax.dot_general(
-                high, basis, NT, preferred_element_type=F32
-            ) + lax.dot_general(low, basis, NT, preferred_element_type=F32)
+    def leaf(group):
+        def add(block, carry):
+            part = jnp.zeros((2 * GW, 2 * NODES), F32)
+            for inner in range(UNROLL):
+                step = block * UNROLL + inner
+                zr = zr_ref[step]
+                zi = zi_ref[step]
+                reals = []
+                imags = []
+                for u in range(group * GU, (group + 1) * GU):
+                    start = HALF * (u % 2) + u // 2
+                    hr = hr_ref[step, start : start + TGT2, :]
+                    hi = hi_ref[step, start : start + TGT2, :]
+                    reals.append(hr * zr - hi * zi)
+                    imags.append(hr * zi + hi * zr)
+                high, low = split(jnp.concatenate(reals + imags, axis=0))
+                basis = basis_ref[step]
+                part = part + jnp.dot(high, basis, preferred_element_type=F32)
+                part = part + jnp.dot(low, basis, preferred_element_type=F32)
+            acc_ref[...] += part
             return carry
 
         acc_ref[...] = jnp.zeros_like(acc_ref)
-        lax.fori_loop(0, steps, add, 0)
+        lax.fori_loop(0, steps // UNROLL, add, 0)
         whole = jnp.transpose(acc_ref[...])
         both = whole[:NODES] + whole[NODES:]
-        return both[:, :CW], both[:, CW:]
+        return [
+            (both[:, i * CW : (i + 1) * CW], both[:, GW + i * CW : GW + (i + 1) * CW])
+            for i in range(GROUP)
+        ]
 
     lane = lax.broadcasted_iota(jnp.int32, (1, CW), 1)
 
@@ -285,12 +338,11 @@
         table_mine = low * (1.0 - side) + high * side
         table_other = low * side + high * (1.0 - side)
         table = jnp.concatenate([table_mine, table_other], axis=1)
-        total = jnp.dot(
-            table,
-            jnp.concatenate(lifted, axis=0),
-            precision=lax.Precision.HIGHEST,
-            preferred_element_type=F32,
-        )
+        table_high, table_low = split(table)
+        high, low = split(jnp.concatenate(lifted, axis=0))
+        total = jnp.dot(table_high, high, preferred_element_type=F32)
+        total = total + jnp.dot(table_low, high, preferred_element_type=F32)
+        total = total + jnp.dot(table_high, low, preferred_element_type=F32)
         return total[:, :CW], total[:, CW:]
 
     def finish(chunk, total):
@@ -318,22 +370,25 @@
         exchange(stage, chunk).start()
 
     greeted = False
-    for slot in range(CHUNKS + 4):
-        if slot < CHUNKS:
-            value = leaf(slot)
+    groups = CHUNKS // GROUP
+    for slot in range(groups + 4):
+        if slot < groups:
+            values = leaf(slot)
             if not greeted:
                 pl.semaphore_wait(barrier, 4)
                 greeted = True
-            send(0, slot, value)
+            for i in range(GROUP):
+                send(0, slot * GROUP + i, values[i])
         for stage in range(3, -1, -1):
-            chunk = slot - 1 - stage
-            if 0 <= chunk < CHUNKS:
-                exchange(stage, chunk).wait()
-                value = merge(chunk, stage, sent_ref.at[stage, chunk], got_ref.at[stage, chunk])
-                if stage < 3:
-                    send(stage + 1, chunk, value)
-                else:
-                    finish(chunk, value)
+            group = slot - 1 - stage
+            if 0 <= group < groups:
+                for chunk in range(group * GROUP, (group + 1) * GROUP):
+                    exchange(stage, chunk).wait()
+                    value = merge(chunk, stage, sent_ref.at[stage, chunk], got_ref.at[stage, chunk])
+                    if stage < 3:
+                        send(stage + 1, chunk, value)
+                    else:
+                        finish(chunk, value)
 
 
 def on_device(point_box, point_offset, point_value, coef):
@@ -345,15 +400,23 @@
     cap = 2 * held // owners
     vmem = pl.BlockSpec(memory_space=pltpu.VMEM)
     tri = jnp.asarray(np.triu(np.ones((256, 256), np.float32), 1), BF16)
-    sent = pl.pallas_call(
-        functools.partial(pack_kernel, owners, cap),
-        out_shape=jax.ShapeDtypeStruct((owners, 4 * cap), F32),
+    block = (owners, 4 * cap // 128, 128)
+    arrived = pl.pallas_call(
+        functools.partial(pack_kernel, boxes_y, owners, cap),
+        out_shape=jax.ShapeDtypeStruct(block, F32),
         in_specs=[vmem] * 4,
         out_specs=vmem,
-        compiler_params=pltpu.CompilerParams(vmem_limit_bytes=16 << 20),
+        scratch_shapes=[
+            pltpu.VMEM(block, F32),
+            pltpu.VMEM(block, F32),
+            pltpu.SemaphoreType.DMA((owners,)),
+            pltpu.SemaphoreType.DMA((owners,)),
+        ],
+        compiler_params=pltpu.CompilerParams(
+            collective_id=1, has_side_effects=True, vmem_limit_bytes=16 << 20
+        ),
         name="pack",
     )(point_box.reshape(1, held), point_offset, point_value, tri)
-    arrived = lax.all_to_all(sent, ("bx", "by"), split_axis=0, concat_axis=0, tiled=True)
     slots = owners * cap
     steps = slots // STEP
     columns = arrived.reshape(owners, 4, cap).transpose(1, 0, 2).reshape(4, steps, STEP)
@@ -370,8 +433,8 @@
             pltpu.VMEM((steps, 2 * HALF, STEP), F32),
             pltpu.VMEM((steps, TGT2, STEP), F32),
             pltpu.VMEM((steps, TGT2, STEP), F32),
-            pltpu.VMEM((steps, 2 * NODES, STEP), BF16),
-            pltpu.VMEM((2 * CW, 2 * NODES), F32),
+            pltpu.VMEM((steps, STEP, 2 * NODES), BF16),
+            pltpu.VMEM((2 * GW, 2 * NODES), F32),
             pltpu.VMEM((4, CHUNKS, 2, NODES, CW), F32),
             pltpu.VMEM((4, CHUNKS, 2, NODES, CW), F32),
             pltpu.SemaphoreType.DMA((4, CHUNKS)),

time: 83.9 us -> 62.5 us (0.74)
  blocking collectives: 14.4 us -> 0 us
  Pallas kernels: 64.4 us -> 57.5 us
    pallas_call x1, Pallas kernels: 63.1 us -> 46.1 us  [on_device(): pl.pallas_call(functools.partial(main_kernel, boxes_x, boxes_y), out_shap...]
    all_to_all x1 -> x0, blocking collectives: 14.4 us -> none  [on_device(): lax.all_to_all(sent, ('bx', 'by'), split_axis=0, concat_axis=0, tiled=True)]
    pallas_call x1, Pallas kernels: 1.34 us -> 11.4 us  [on_device(): pl.pallas_call(functools.partial(pack_kernel, boxes_y, owners, cap), out_...]
where the time goes in v2:
time: 62.5 us; the launch traced here: 62.1 us
  Pallas kernels  57.5 us (92%)
  local copies, waits for them, and re-layouts  4.46 us (7%)
    pallas_call x1, Pallas kernels, on_device(): pl.pallas_call(functools.partial(main_kernel, boxes_x, boxes_y), out_shap...  46.1 us
    pallas_call x1, Pallas kernels, on_device(): pl.pallas_call(functools.partial(pack_kernel, boxes_y, owners, cap), out_...  11.4 us
    unnamed x17, local copies, waits for them, and re-layouts  4.46 us

profile of v2, /device:TPU:0, one launch (start us, length us, event | category | flops | bytes accessed | tf_op | source)
XLA Modules:
  0.0 62.1 jit_solution(14728871461017062647)
XLA Ops:
  0.0 0.0 copy-start
  0.0 0.9 %copy-done = bf16[256,256]{1,0:T(8,128)(2,1)S(1)} copy-done((bf16[256,256]{1,0:T(8,128)(2,1)S(1)}, bf16[256,256]{1,0:T(8,128)(2,1)}, u32[]{:S(2)}) %copy-start) | copy-done | bytes 131096
  0.9 0.0 copy-start.3
  0.9 0.7 %copy-done.3 = s32[2,2048]{1,0:T(2,128)S(1)} copy-done((s32[2,2048]{1,0:T(2,128)S(1)}, s32[2,2048]{1,0:T(2,128)}, u32[]{:S(2)}) %copy-start.3) | copy-done | bytes 16408
  1.6 0.0 copy-start.4
  1.6 0.7 %copy-done.4 = f32[2,2048]{1,0:T(2,128)S(1)} copy-done((f32[2,2048]{1,0:T(2,128)S(1)}, f32[2,2048]{1,0:T(2,128)}, u32[]{:S(2)}) %copy-start.4) | copy-done | bytes 16408
  2.3 0.0 copy-start.5
  2.3 0.7 %copy-done.5 = s32[2048,1]{0,1:T(1,128)S(1)} copy-done((s32[2048,1]{0,1:T(1,128)S(1)}, s32[2048,1]{0,1:T(1,128)}, u32[]{:S(2)}) %copy-start.5) | copy-done | bytes 8216
  3.0 0.0 copy-start.1
  3.0 0.0 copy-start.2
  3.0 0.0 copy-start.6
  3.0 11.4 %pack.1 = f32[32,4,128]{2,1,0:T(4,128)S(1)} custom-call(s32[1,2048]{1,0:T(1,128)S(1)} %bitcast.7, s32[2,2048]{1,0:T(2,128)S(1)} %copy-done.3, f32[2,2048]{1,0:T(2,128)S(1)} %copy-done.4, bf16[256,256]{1,0:T(8,128)(2,1)S(1)} %copy-done), custom_call_target="tpu_custom_call" | custom-call | tf_op jit(solution)/shard_map/pack/pallas_call | solution.py:404
  14.5 0.0 copy-start.7
  14.5 0.0 copy-done.1
  14.5 0.0 copy-done.2
  14.5 0.0 copy-done.6
  14.5 0.6 copy-done.7
  15.1 46.1 %butterfly.1 = f32[2,64,1024]{2,1,0:T(8,128)S(1)} custom-call(s32[4]{0:T(128)S(1)} %copy-done.7, f32[16,4,256]{2,1,0:T(4,128)S(1)} %bitcast.6, f32[2,2,64,64]{3,2,1,0:T(8,128)S(1)} %copy-done.1, f32[8,8]{1,0:T(8,128)S(1)} %copy-done.6, f32[64,2]{1,0:T(8,128)S(1)} %copy-done.2), custom_call_target="tpu_custom_call" | custom-call | tf_op jit(solution)/shard_map/butterfly/pallas_call | solution.py:426
  61.3 0.8 %copy.10 = f32[2,64,1024]{2,1,0:T(8,128)} copy(f32[2,64,1024]{2,1,0:T(8,128)S(1)} %butterfly.1) | data formatting | bytes 1048576
Async XLA Ops:
  0.0 0.9 %copy-start = (bf16[256,256]{1,0:T(8,128)(2,1)S(1)}, bf16[256,256]{1,0:T(8,128)(2,1)}, u32[]{:S(2)}) copy-start(bf16[256,256]{1,0:T(8,128)(2,1)} %constant.8.clone.tri_ref) | copy-start | bytes 393220
  0.9 0.7 %copy-start.3 = (s32[2,2048]{1,0:T(2,128)S(1)}, s32[2,2048]{1,0:T(2,128)}, u32[]{:S(2)}) copy-start(s32[2,2048]{1,0:T(2,128)} %offset_ref.1) | copy-start | bytes 49156
  1.6 0.7 %copy-start.4 = (f32[2,2048]{1,0:T(2,128)S(1)}, f32[2,2048]{1,0:T(2,128)}, u32[]{:S(2)}) copy-start(f32[2,2048]{1,0:T(2,128)} %value_ref.1) | copy-start | bytes 49156
  2.3 0.7 %copy-start.5 = (s32[2048,1]{0,1:T(1,128)S(1)}, s32[2048,1]{0,1:T(1,128)}, u32[]{:S(2)}) copy-start(s32[2048,1]{0,1:T(1,128)} %param.8) | copy-start | bytes 24580
  3.0 11.4 %copy-start.1 = (f32[2,2,64,64]{3,2,1,0:T(8,128)S(1)}, f32[2,2,64,64]{3,2,1,0:T(8,128)}, u32[]{:S(2)}) copy-start(f32[2,2,64,64]{3,2,1,0:T(8,128)} %constant.9.clone.merge_ref) | copy-start | bytes 196612
  3.0 11.4 %copy-start.2 = (f32[64,2]{1,0:T(8,128)S(1)}, f32[64,2]{1,0:T(8,128)}, u32[]{:S(2)}) copy-start(f32[64,2]{1,0:T(8,128)} %constant.11.clone.node_ref) | copy-start | bytes 1540
  3.0 11.5 %copy-start.6 = (f32[8,8]{1,0:T(8,128)S(1)}, f32[8,8]{1,0:T(8,128)}, u32[]{:S(2)}) copy-start(f32[8,8]{1,0:T(8,128)} %constant.10.clone.scale_ref) | copy-start | bytes 772
  14.5 0.7 %copy-start.7 = (s32[4]{0:T(128)S(1)}, s32[4]{0:T(128)}, u32[]{:S(2)}) copy-start(s32[4]{0:T(128)} %coef_ref.1) | copy-start | bytes 52

commit v3 on v2

--- a/solution.py
+++ b/solution.py
@@ -18,8 +18,8 @@
 CW = UC * TGT2
 CHUNKS = TGT1 // UC
 GROUP = 2
-GU = GROUP * UC
-GW = GROUP * CW
+GROUPS = CHUNKS // GROUP
+WRAP = 24
 UNROLL = 2
 HALF = 48
 MESH = pl.DeviceIdType.MESH
@@ -94,11 +94,18 @@
 
 
 def pack_kernel(
-    boxes_y, owners, cap, ids_ref, offset_ref, value_ref, tri_ref, out_ref,
-    sent_ref, got_ref, send_sem, recv_sem,
+    boxes_y, owners, cap, ids_hbm, offset_hbm, value_hbm, out_ref,
+    ids_ref, offset_ref, value_ref, sent_ref, got_ref, load_sem, send_sem, recv_sem,
 ):
     me = lax.axis_index("bx") * boxes_y + lax.axis_index("by")
     barrier = pltpu.get_barrier_semaphore()
+    loads = [
+        pltpu.make_async_copy(ids_hbm, ids_ref, load_sem.at[0]),
+        pltpu.make_async_copy(offset_hbm, offset_ref, load_sem.at[1]),
+        pltpu.make_async_copy(value_hbm, value_ref, load_sem.at[2]),
+    ]
+    for load in loads:
+        load.start()
 
     def place_of(distance):
         target = (me + distance) % owners
@@ -112,14 +119,19 @@
     lax.fori_loop(1, owners, greet, 0)
     total = ids_ref.shape[1]
     width = 256
+    earlier = lax.broadcasted_iota(jnp.int32, (width, width), 0)
+    later = lax.broadcasted_iota(jnp.int32, (width, width), 1)
+    tri = (earlier < later).astype(F32).astype(BF16)
     carry = jnp.zeros((owners, 1), F32)
+    for load in loads:
+        load.wait()
     packed = jnp.zeros((10 * owners, cap), F32)
     for block in range(total // width):
         lanes = slice(block * width, (block + 1) * width)
         ids = ids_ref[:, lanes]
         hit = ids == lax.broadcasted_iota(jnp.int32, (owners, width), 0)
         onehot = hit.astype(F32)
-        before = jnp.dot(onehot.astype(BF16), tri_ref[...], preferred_element_type=F32) + carry
+        before = jnp.dot(onehot.astype(BF16), tri, preferred_element_type=F32) + carry
         ranks = jnp.sum(before * onehot, axis=0, keepdims=True)
         carry = carry + jnp.sum(onehot, axis=1, keepdims=True)
         slot = lax.broadcasted_iota(jnp.int32, (cap, width), 0)
@@ -182,7 +194,7 @@
 
 
 def main_kernel(
-    boxes_x, boxes_y, coef_ref, col_ref, merge_ref, scale_ref, node_ref, out_ref,
+    boxes_x, boxes_y, coef_ref, col_ref, merge_ref, out_ref,
     hr_ref, hi_ref, zr_ref, zi_ref, basis_ref, acc_ref, sent_ref, got_ref, send_sem, recv_sem,
 ):
     ix = lax.axis_index("bx")
@@ -213,17 +225,35 @@
     sq_first = speed_first * speed_first
     sq_second = speed_second * speed_second
     m_scale = (2.0 * m + 1.0) * (boxes_x / (2.0 * N))
-    v_scale = lax.broadcasted_iota(jnp.int32, (TGT2, 1), 0).astype(F32) * (boxes_y / N)
+    v_row = lax.broadcasted_iota(jnp.int32, (TGT2, 1), 0)
+    unit = boxes_y / N
+    v_first = (v_row + 4).astype(F32) * unit
+    v_second = jnp.where(v_row < WRAP, v_row + 4, v_row - 12).astype(F32) * unit
     half_turn = ((ix + iy) % 2).astype(F32) * 0.5
     corner_first = (ix * wx).astype(F32)
     corner_second = (iy * wy).astype(F32)
     node_values = node_table()
     order_row = lax.broadcasted_iota(jnp.int32, (ORDER, 1), 0)
 
+    scales = lagrange_scales()
+
+    def column(values):
+        chosen = jnp.full((ORDER, 1), float(values[0]), F32)
+        for i in range(1, ORDER):
+            chosen = jnp.where(order_row == i, float(values[i]), chosen)
+        return chosen
+
+    scale_columns = [column(scales[:, source]) for source in range(ORDER)]
+    tile_nodes = column(node_values)
+    second_nodes = jnp.concatenate([tile_nodes] * ORDER, axis=0)
+    first_nodes = jnp.concatenate(
+        [jnp.full((ORDER, 1), float(node_values[t]), F32) for t in range(ORDER)], axis=0
+    )
+
     def lagrange(coords):
         factor = jnp.ones((ORDER, STEP), F32)
         for source in range(ORDER):
-            term = (coords - float(node_values[source])) * scale_ref[:, source : source + 1]
+            term = (coords - float(node_values[source])) * scale_columns[source]
             factor = factor * jnp.where(order_row == source, 1.0, term)
         return factor
 
@@ -239,49 +269,71 @@
         cosine, sine = cos_sin((linear - jnp.round(linear)) + root)
         hr_ref[step] = cosine * re - sine * im
         hi_ref[step] = cosine * im + sine * re
-        cosine, sine = cos_sin(v_scale * (o2 - o1))
+        cosine, sine = cos_sin(v_second * o2 - v_first * o1)
         zr_ref[step] = cosine
         zi_ref[step] = sine
         first = lagrange(o1 * (1.0 / wx))
         second = lagrange(o2 * (1.0 / wy))
         basis = jnp.concatenate([first[t : t + 1] * second for t in range(ORDER)], axis=0)
-        high, low = split(basis)
-        both = jnp.concatenate([high.astype(F32), low.astype(F32)], axis=0)
-        basis_ref[step] = jnp.transpose(both).astype(BF16)
+        half_turns = (4.0 * unit * (o2 - o1), -unit * (4.0 * o1 + 12.0 * o2))
+        for side, cycles in enumerate(half_turns):
+            cosine, sine = cos_sin(cycles)
+            high, low = split(jnp.concatenate([basis * cosine, basis * sine], axis=0))
+            basis_ref[side, step] = jnp.transpose(jnp.concatenate([high, low], axis=0))
         return carry
 
     lax.fori_loop(0, steps, tables, 0)
 
     def leaf(group):
+        first_u = TGT1 // 2 + group * UC
+        spans = (slice(0, WRAP), slice(WRAP, TGT2))
+
         def add(block, carry):
-            part = jnp.zeros((2 * GW, 2 * NODES), F32)
+            parts = [0.0, 0.0]
             for inner in range(UNROLL):
                 step = block * UNROLL + inner
-                zr = zr_ref[step]
-                zi = zi_ref[step]
-                reals = []
-                imags = []
-                for u in range(group * GU, (group + 1) * GU):
-                    start = HALF * (u % 2) + u // 2
-                    hr = hr_ref[step, start : start + TGT2, :]
-                    hi = hi_ref[step, start : start + TGT2, :]
-                    reals.append(hr * zr - hi * zi)
-                    imags.append(hr * zi + hi * zr)
-                high, low = split(jnp.concatenate(reals + imags, axis=0))
-                basis = basis_ref[step]
-                part = part + jnp.dot(high, basis, preferred_element_type=F32)
-                part = part + jnp.dot(low, basis, preferred_element_type=F32)
-            acc_ref[...] += part
+                for side, span in enumerate(spans):
+                    zr = zr_ref[step, span, :]
+                    zi = zi_ref[step, span, :]
+                    reals = []
+                    imags = []
+                    for u in range(first_u, first_u + UC):
+                        start = HALF * (u % 2) + u // 2
+                        hr = hr_ref[step, start + span.start : start + span.stop, :]
+                        hi = hi_ref[step, start + span.start : start + span.stop, :]
+                        reals.append(hr * zr - hi * zi)
+                        imags.append(hr * zi + hi * zr)
+                    high, low = split(jnp.concatenate(reals + imags, axis=0))
+                    basis = basis_ref[side, step]
+                    part = jnp.dot(high, basis, preferred_element_type=F32)
+                    part = part + jnp.dot(low, basis, preferred_element_type=F32)
+                    parts[side] = parts[side] + part
+            acc_ref[: 2 * UC * WRAP] += parts[0]
+            acc_ref[2 * UC * WRAP :] += parts[1]
             return carry
 
         acc_ref[...] = jnp.zeros_like(acc_ref)
         lax.fori_loop(0, steps // UNROLL, add, 0)
-        whole = jnp.transpose(acc_ref[...])
-        both = whole[:NODES] + whole[NODES:]
-        return [
-            (both[:, i * CW : (i + 1) * CW], both[:, GW + i * CW : GW + (i + 1) * CW])
-            for i in range(GROUP)
-        ]
+        summed = acc_ref[:, : 2 * NODES] + acc_ref[:, 2 * NODES :]
+        rest = TGT2 - WRAP
+        same = []
+        turned = []
+        for i in range(2 * UC):
+            head = summed[i * WRAP : (i + 1) * WRAP]
+            tail = summed[2 * UC * WRAP + i * rest : 2 * UC * WRAP + (i + 1) * rest]
+            same += [head, tail]
+            turned += [tail, head]
+        same = jnp.transpose(jnp.concatenate(same, axis=0))
+        turned = jnp.transpose(jnp.concatenate(turned, axis=0))
+        upper = (
+            same[:NODES, :CW] + same[NODES:, CW:],
+            same[:NODES, CW:] - same[NODES:, :CW],
+        )
+        lower = (
+            turned[:NODES, :CW] - turned[NODES:, CW:],
+            turned[:NODES, CW:] + turned[NODES:, :CW],
+        )
+        return {group: lower, GROUPS + group: upper}
 
     lane = lax.broadcasted_iota(jnp.int32, (1, CW), 1)
 
@@ -300,8 +352,8 @@
     def box_nodes(px, py, m1, m2):
         a1 = (px // 2**m1 * (wx * 2**m1)).astype(F32)
         a2 = (py // 2**m2 * (wy * 2**m2)).astype(F32)
-        n1 = a1 + float(wx * 2**m1) * node_ref[:, 0:1]
-        n2 = a2 + float(wy * 2**m2) * node_ref[:, 1:2]
+        n1 = a1 + float(wx * 2**m1) * first_nodes
+        n2 = a2 + float(wy * 2**m2) * second_nodes
         return n1, n2
 
     def merge(chunk, stage, mine, other):
@@ -370,19 +422,18 @@
         exchange(stage, chunk).start()
 
     greeted = False
-    groups = CHUNKS // GROUP
-    for slot in range(groups + 4):
-        if slot < groups:
+    for slot in range(GROUPS + 4):
+        if slot < GROUPS:
             values = leaf(slot)
             if not greeted:
                 pl.semaphore_wait(barrier, 4)
                 greeted = True
-            for i in range(GROUP):
-                send(0, slot * GROUP + i, values[i])
+            for chunk, value in values.items():
+                send(0, chunk, value)
         for stage in range(3, -1, -1):
             group = slot - 1 - stage
-            if 0 <= group < groups:
-                for chunk in range(group * GROUP, (group + 1) * GROUP):
+            if 0 <= group < GROUPS:
+                for chunk in (group, GROUPS + group):
                     exchange(stage, chunk).wait()
                     value = merge(chunk, stage, sent_ref.at[stage, chunk], got_ref.at[stage, chunk])
                     if stage < 3:
@@ -399,16 +450,19 @@
     held = point_box.shape[0]
     cap = 2 * held // owners
     vmem = pl.BlockSpec(memory_space=pltpu.VMEM)
-    tri = jnp.asarray(np.triu(np.ones((256, 256), np.float32), 1), BF16)
     block = (owners, 4 * cap // 128, 128)
     arrived = pl.pallas_call(
         functools.partial(pack_kernel, boxes_y, owners, cap),
         out_shape=jax.ShapeDtypeStruct(block, F32),
-        in_specs=[vmem] * 4,
+        in_specs=[pl.BlockSpec(memory_space=pl.ANY)] * 3,
         out_specs=vmem,
         scratch_shapes=[
+            pltpu.VMEM((1, held), jnp.int32),
+            pltpu.VMEM((2, held), jnp.int32),
+            pltpu.VMEM((2, held), F32),
             pltpu.VMEM(block, F32),
             pltpu.VMEM(block, F32),
+            pltpu.SemaphoreType.DMA((3,)),
             pltpu.SemaphoreType.DMA((owners,)),
             pltpu.SemaphoreType.DMA((owners,)),
         ],
@@ -416,25 +470,23 @@
             collective_id=1, has_side_effects=True, vmem_limit_bytes=16 << 20
         ),
         name="pack",
-    )(point_box.reshape(1, held), point_offset, point_value, tri)
+    )(point_box.reshape(1, held), point_offset, point_value)
     slots = owners * cap
     steps = slots // STEP
     columns = arrived.reshape(owners, 4, cap).transpose(1, 0, 2).reshape(4, steps, STEP)
     columns = columns.transpose(1, 0, 2)
-    nodes = node_table().astype(np.float32)
-    node_pairs = np.stack([np.repeat(nodes, ORDER), np.tile(nodes, ORDER)], axis=1)
     return pl.pallas_call(
         functools.partial(main_kernel, boxes_x, boxes_y),
         out_shape=jax.ShapeDtypeStruct((2, NODES, TGT1 * TGT2), F32),
-        in_specs=[pl.BlockSpec(memory_space=pltpu.SMEM)] + [vmem] * 4,
+        in_specs=[pl.BlockSpec(memory_space=pltpu.SMEM)] + [vmem] * 2,
         out_specs=vmem,
         scratch_shapes=[
             pltpu.VMEM((steps, 2 * HALF, STEP), F32),
             pltpu.VMEM((steps, 2 * HALF, STEP), F32),
             pltpu.VMEM((steps, TGT2, STEP), F32),
             pltpu.VMEM((steps, TGT2, STEP), F32),
-            pltpu.VMEM((steps, STEP, 2 * NODES), BF16),
-            pltpu.VMEM((2 * GW, 2 * NODES), F32),
+            pltpu.VMEM((2, steps, STEP, 4 * NODES), BF16),
+            pltpu.VMEM((2 * CW, 4 * NODES), F32),
             pltpu.VMEM((4, CHUNKS, 2, NODES, CW), F32),
             pltpu.VMEM((4, CHUNKS, 2, NODES, CW), F32),
             pltpu.SemaphoreType.DMA((4, CHUNKS)),
@@ -444,7 +496,7 @@
             collective_id=0, has_side_effects=True, vmem_limit_bytes=40 << 20
         ),
         name="butterfly",
-    )(coef, columns, jnp.asarray(merge_tables()), jnp.asarray(lagrange_scales()), jnp.asarray(node_pairs))
+    )(coef, columns, jnp.asarray(merge_tables()))
 
 
 def solution(mesh):

time: 62.5 us -> 57.6 us (0.922)
  Pallas kernels: 57.5 us -> 52.7 us
    pallas_call x1, Pallas kernels: 46.1 us -> 41.2 us  [on_device(): pl.pallas_call(functools.partial(main_kernel, boxes_x, boxes_y), out_shap...]
    unnamed x17 -> x11, local copies, waits for them, and re-layouts: 4.46 us -> 4.48 us
where the time goes in v3:
time: 57.6 us; the launch traced here: 57.2 us
  Pallas kernels  52.7 us (91%)
  local copies, waits for them, and re-layouts  4.48 us (8%)
    pallas_call x1, Pallas kernels, on_device(): pl.pallas_call(functools.partial(main_kernel, boxes_x, boxes_y), out_shap...  41.2 us
    pallas_call x1, Pallas kernels, on_device(): pl.pallas_call(functools.partial(pack_kernel, boxes_y, owners, cap), out_...  11.6 us
    unnamed x11, local copies, waits for them, and re-layouts  4.48 us

profile of v3, /device:TPU:0, one launch (start us, length us, event | category | flops | bytes accessed | tf_op | source)
XLA Modules:
  0.0 57.2 jit_solution(2022785828220562007)
XLA Ops:
  0.0 0.0 copy-start.1
  0.0 0.7 %copy-done.1 = s32[2,2048]{1,0:T(2,128)S(1)} copy-done((s32[2,2048]{1,0:T(2,128)S(1)}, s32[2,2048]{1,0:T(2,128)}, u32[]{:S(2)}) %copy-start.1) | copy-done | bytes 16408
  0.7 0.0 copy-start.2
  0.7 0.7 %copy-done.2 = f32[2,2048]{1,0:T(2,128)S(1)} copy-done((f32[2,2048]{1,0:T(2,128)S(1)}, f32[2,2048]{1,0:T(2,128)}, u32[]{:S(2)}) %copy-start.2) | copy-done | bytes 16408
  1.4 0.0 copy-start.3
  1.4 0.7 %copy-done.3 = s32[2048,1]{0,1:T(1,128)S(1)} copy-done((s32[2048,1]{0,1:T(1,128)S(1)}, s32[2048,1]{0,1:T(1,128)}, u32[]{:S(2)}) %copy-start.3) | copy-done | bytes 8216
  2.1 11.6 %pack.1 = f32[32,4,128]{2,1,0:T(4,128)S(1)} custom-call(s32[1,2048]{1,0:T(1,128)S(1)} %bitcast.7, s32[2,2048]{1,0:T(2,128)S(1)} %copy-done.1, f32[2,2048]{1,0:T(2,128)S(1)} %copy-done.2), custom_call_target="tpu_custom_call" | custom-call | tf_op jit(solution)/shard_map/pack/pallas_call | solution.py:454
  13.7 0.0 copy-start.4
  13.7 0.6 %copy-done.4 = s32[4]{0:T(128)S(1)} copy-done((s32[4]{0:T(128)S(1)}, s32[4]{0:T(128)}, u32[]{:S(2)}) %copy-start.4) | copy-done | bytes 40
  14.4 0.0 copy-start
  14.4 0.9 %copy-done = f32[2,2,64,64]{3,2,1,0:T(8,128)S(1)} copy-done((f32[2,2,64,64]{3,2,1,0:T(8,128)S(1)}, f32[2,2,64,64]{3,2,1,0:T(8,128)}, u32[]{:S(2)}) %copy-start) | copy-done | bytes 65560
  15.3 41.2 %butterfly.1 = f32[2,64,1024]{2,1,0:T(8,128)S(1)} custom-call(s32[4]{0:T(128)S(1)} %copy-done.4, f32[16,4,256]{2,1,0:T(4,128)S(1)} %bitcast.6, f32[2,2,64,64]{3,2,1,0:T(8,128)S(1)} %copy-done), custom_call_target="tpu_custom_call" | custom-call | tf_op jit(solution)/shard_map/butterfly/pallas_call | solution.py:478
  56.4 0.8 %copy.7 = f32[2,64,1024]{2,1,0:T(8,128)} copy(f32[2,64,1024]{2,1,0:T(8,128)S(1)} %butterfly.1) | data formatting | bytes 1048576
Async XLA Ops:
  0.0 0.7 %copy-start.1 = (s32[2,2048]{1,0:T(2,128)S(1)}, s32[2,2048]{1,0:T(2,128)}, u32[]{:S(2)}) copy-start(s32[2,2048]{1,0:T(2,128)} %offset_hbm.1) | copy-start | bytes 49156
  0.7 0.7 %copy-start.2 = (f32[2,2048]{1,0:T(2,128)S(1)}, f32[2,2048]{1,0:T(2,128)}, u32[]{:S(2)}) copy-start(f32[2,2048]{1,0:T(2,128)} %value_hbm.1) | copy-start | bytes 49156
  1.4 0.7 %copy-start.3 = (s32[2048,1]{0,1:T(1,128)S(1)}, s32[2048,1]{0,1:T(1,128)}, u32[]{:S(2)}) copy-start(s32[2048,1]{0,1:T(1,128)} %param.5) | copy-start | bytes 24580
  13.7 0.7 %copy-start.4 = (s32[4]{0:T(128)S(1)}, s32[4]{0:T(128)}, u32[]{:S(2)}) copy-start(s32[4]{0:T(128)} %coef_ref.1) | copy-start | bytes 52
  14.4 0.9 %copy-start = (f32[2,2,64,64]{3,2,1,0:T(8,128)S(1)}, f32[2,2,64,64]{3,2,1,0:T(8,128)}, u32[]{:S(2)}) copy-start(f32[2,2,64,64]{3,2,1,0:T(8,128)} %constant.2.clone.merge_ref) | copy-start | bytes 196612

commit v4 on v3

--- a/solution.py
+++ b/solution.py
@@ -195,7 +195,7 @@
 
 def main_kernel(
     boxes_x, boxes_y, coef_ref, col_ref, merge_ref, out_ref,
-    hr_ref, hi_ref, zr_ref, zi_ref, basis_ref, acc_ref, sent_ref, got_ref, send_sem, recv_sem,
+    hr_ref, hi_ref, zr_ref, zi_ref, basis_ref, acc_ref, ratio_ref, sent_ref, got_ref, send_sem, recv_sem,
 ):
     ix = lax.axis_index("bx")
     iy = lax.axis_index("by")
@@ -356,12 +356,12 @@
         n2 = a2 + float(wy * 2**m2) * second_nodes
         return n1, n2
 
-    def merge(chunk, stage, mine, other):
+    def ratios(stage):
         level, along = stage // 2, stage % 2
         m1, m2 = level + along, level
         new1, new2 = (m1 + 1, m2) if along == 0 else (m1, m2 + 1)
-        old_place = centre(chunk, m1, m2)
-        new_place = centre(chunk, new1, new2)
+        old_place = centre(0, m1, m2)
+        new_place = centre(0, new1, new2)
         shift1 = (
             (code_of(ix, new1).astype(F32) + 0.5) * (boxes_x / (N * 2.0**new1))
             - (code_of(ix, m1).astype(F32) + 0.5) * (boxes_x / (N * 2.0**m1))
@@ -372,13 +372,30 @@
         )
         px = flipped(ix, level) if along == 0 else ix
         py = flipped(iy, level) if along == 1 else iy
-        bit = ((ix if along == 0 else iy) // 2**level) % 2
-        lifted = []
-        for child, bx, by in ((mine, ix, iy), (other, px, py)):
+        for child, (bx, by) in enumerate(((ix, iy), (px, py))):
             n1, n2 = box_nodes(bx, by, m1, m2)
             linear = shift1 * n1 + shift2 * n2
             cycles = (roots(new_place, n1, n2) - roots(old_place, n1, n2)) + linear
             cosine, sine = cos_sin(cycles)
+            ratio_ref[stage, child, 0] = cosine
+            ratio_ref[stage, child, 1] = sine
+
+    def turned_ratio(stage, child, chunk):
+        turn = 2 * chunk
+        for part in range(2):
+            value = ratio_ref[stage, child, part]
+            if turn:
+                near = pltpu.roll(value, CW - turn, 1)
+                far = pltpu.roll(value, TGT2 - turn, 1)
+                value = jnp.where(lane % TGT2 + turn < TGT2, near, far)
+            yield value
+
+    def merge(chunk, stage, mine, other):
+        level, along = stage // 2, stage % 2
+        bit = ((ix if along == 0 else iy) // 2**level) % 2
+        lifted = []
+        for index, child in enumerate((mine, other)):
+            cosine, sine = turned_ratio(stage, index, chunk)
             lifted.append(
                 jnp.concatenate(
                     [cosine * child[0] - sine * child[1], cosine * child[1] + sine * child[0]],
@@ -421,6 +438,8 @@
         sent_ref[stage, chunk, 1] = value[1]
         exchange(stage, chunk).start()
 
+    for stage in range(4):
+        ratios(stage)
     greeted = False
     for slot in range(GROUPS + 4):
         if slot < GROUPS:
@@ -487,6 +506,7 @@
             pltpu.VMEM((steps, TGT2, STEP), F32),
             pltpu.VMEM((2, steps, STEP, 4 * NODES), BF16),
             pltpu.VMEM((2 * CW, 4 * NODES), F32),
+            pltpu.VMEM((4, 2, 2, NODES, CW), F32),
             pltpu.VMEM((4, CHUNKS, 2, NODES, CW), F32),
             pltpu.VMEM((4, CHUNKS, 2, NODES, CW), F32),
             pltpu.SemaphoreType.DMA((4, CHUNKS)),

time: 57.6 us -> 57.8 us (level)
  no operation moved by 1% of the time
where the time goes in v4:
time: 57.8 us; the launch traced here: 57.4 us
  Pallas kernels  52.9 us (92%)
  local copies, waits for them, and re-layouts  4.48 us (8%)
    pallas_call x1, Pallas kernels, on_device(): pl.pallas_call(functools.partial(main_kernel, boxes_x, boxes_y), out_shap...  41.3 us
    pallas_call x1, Pallas kernels, on_device(): pl.pallas_call(functools.partial(pack_kernel, boxes_y, owners, cap), out_...  11.6 us
    unnamed x11, local copies, waits for them, and re-layouts  4.48 us

profile of v4, /device:TPU:0, one launch (start us, length us, event | category | flops | bytes accessed | tf_op | source)
XLA Modules:
  0.0 57.4 jit_solution(5501735390053051657)
XLA Ops:
  0.0 0.0 copy-start.1
  0.0 0.7 %copy-done.1 = s32[2,2048]{1,0:T(2,128)S(1)} copy-done((s32[2,2048]{1,0:T(2,128)S(1)}, s32[2,2048]{1,0:T(2,128)}, u32[]{:S(2)}) %copy-start.1) | copy-done | bytes 16408
  0.7 0.0 copy-start.2
  0.7 0.7 %copy-done.2 = f32[2,2048]{1,0:T(2,128)S(1)} copy-done((f32[2,2048]{1,0:T(2,128)S(1)}, f32[2,2048]{1,0:T(2,128)}, u32[]{:S(2)}) %copy-start.2) | copy-done | bytes 16408
  1.4 0.0 copy-start.3
  1.4 0.7 %copy-done.3 = s32[2048,1]{0,1:T(1,128)S(1)} copy-done((s32[2048,1]{0,1:T(1,128)S(1)}, s32[2048,1]{0,1:T(1,128)}, u32[]{:S(2)}) %copy-start.3) | copy-done | bytes 8216
  2.1 11.6 %pack.1 = f32[32,4,128]{2,1,0:T(4,128)S(1)} custom-call(s32[1,2048]{1,0:T(1,128)S(1)} %bitcast.7, s32[2,2048]{1,0:T(2,128)S(1)} %copy-done.1, f32[2,2048]{1,0:T(2,128)S(1)} %copy-done.2), custom_call_target="tpu_custom_call" | custom-call | tf_op jit(solution)/shard_map/pack/pallas_call | solution.py:473
  13.7 0.0 copy-start.4
  13.7 0.6 %copy-done.4 = s32[4]{0:T(128)S(1)} copy-done((s32[4]{0:T(128)S(1)}, s32[4]{0:T(128)}, u32[]{:S(2)}) %copy-start.4) | copy-done | bytes 40
  14.4 0.0 copy-start
  14.4 0.9 %copy-done = f32[2,2,64,64]{3,2,1,0:T(8,128)S(1)} copy-done((f32[2,2,64,64]{3,2,1,0:T(8,128)S(1)}, f32[2,2,64,64]{3,2,1,0:T(8,128)}, u32[]{:S(2)}) %copy-start) | copy-done | bytes 65560
  15.3 41.3 %butterfly.1 = f32[2,64,1024]{2,1,0:T(8,128)S(1)} custom-call(s32[4]{0:T(128)S(1)} %copy-done.4, f32[16,4,256]{2,1,0:T(4,128)S(1)} %bitcast.6, f32[2,2,64,64]{3,2,1,0:T(8,128)S(1)} %copy-done), custom_call_target="tpu_custom_call" | custom-call | tf_op jit(solution)/shard_map/butterfly/pallas_call | solution.py:497
  56.6 0.8 %copy.7 = f32[2,64,1024]{2,1,0:T(8,128)} copy(f32[2,64,1024]{2,1,0:T(8,128)S(1)} %butterfly.1) | data formatting | bytes 1048576
Async XLA Ops:
  0.0 0.7 %copy-start.1 = (s32[2,2048]{1,0:T(2,128)S(1)}, s32[2,2048]{1,0:T(2,128)}, u32[]{:S(2)}) copy-start(s32[2,2048]{1,0:T(2,128)} %offset_hbm.1) | copy-start | bytes 49156
  0.7 0.7 %copy-start.2 = (f32[2,2048]{1,0:T(2,128)S(1)}, f32[2,2048]{1,0:T(2,128)}, u32[]{:S(2)}) copy-start(f32[2,2048]{1,0:T(2,128)} %value_hbm.1) | copy-start | bytes 49156
  1.4 0.7 %copy-start.3 = (s32[2048,1]{0,1:T(1,128)S(1)}, s32[2048,1]{0,1:T(1,128)}, u32[]{:S(2)}) copy-start(s32[2048,1]{0,1:T(1,128)} %param.5) | copy-start | bytes 24580
  13.7 0.7 %copy-start.4 = (s32[4]{0:T(128)S(1)}, s32[4]{0:T(128)}, u32[]{:S(2)}) copy-start(s32[4]{0:T(128)} %coef_ref.1) | copy-start | bytes 52
  14.4 0.9 %copy-start = (f32[2,2,64,64]{3,2,1,0:T(8,128)S(1)}, f32[2,2,64,64]{3,2,1,0:T(8,128)}, u32[]{:S(2)}) copy-start(f32[2,2,64,64]{3,2,1,0:T(8,128)} %constant.2.clone.merge_ref) | copy-start | bytes 196612

commit v5 on v4

--- a/solution.py
+++ b/solution.py
@@ -20,7 +20,7 @@
 GROUP = 2
 GROUPS = CHUNKS // GROUP
 WRAP = 24
-UNROLL = 2
+UNROLL = 4
 HALF = 48
 MESH = pl.DeviceIdType.MESH
 F32 = jnp.float32

time: 57.8 us -> 56.2 us (0.972)
  Pallas kernels: 52.9 us -> 51.3 us
    pallas_call x1, Pallas kernels: 41.3 us -> 39.7 us  [on_device(): pl.pallas_call(functools.partial(main_kernel, boxes_x, boxes_y), out_shap...]
where the time goes in v5:
time: 56.2 us; the launch traced here: 55.8 us
  Pallas kernels  51.3 us (91%)
  local copies, waits for them, and re-layouts  4.48 us (8%)
    pallas_call x1, Pallas kernels, on_device(): pl.pallas_call(functools.partial(main_kernel, boxes_x, boxes_y), out_shap...  39.7 us
    pallas_call x1, Pallas kernels, on_device(): pl.pallas_call(functools.partial(pack_kernel, boxes_y, owners, cap), out_...  11.6 us
    unnamed x11, local copies, waits for them, and re-layouts  4.48 us

profile of v5, /device:TPU:0, one launch (start us, length us, event | category | flops | bytes accessed | tf_op | source)
XLA Modules:
  0.0 55.8 jit_solution(17424885645470780010)
XLA Ops:
  0.0 0.0 copy-start.1
  0.0 0.7 %copy-done.1 = s32[2,2048]{1,0:T(2,128)S(1)} copy-done((s32[2,2048]{1,0:T(2,128)S(1)}, s32[2,2048]{1,0:T(2,128)}, u32[]{:S(2)}) %copy-start.1) | copy-done | bytes 16408
  0.7 0.0 copy-start.2
  0.7 0.7 %copy-done.2 = f32[2,2048]{1,0:T(2,128)S(1)} copy-done((f32[2,2048]{1,0:T(2,128)S(1)}, f32[2,2048]{1,0:T(2,128)}, u32[]{:S(2)}) %copy-start.2) | copy-done | bytes 16408
  1.4 0.0 copy-start.3
  1.4 0.7 %copy-done.3 = s32[2048,1]{0,1:T(1,128)S(1)} copy-done((s32[2048,1]{0,1:T(1,128)S(1)}, s32[2048,1]{0,1:T(1,128)}, u32[]{:S(2)}) %copy-start.3) | copy-done | bytes 8216
  2.1 11.6 %pack.1 = f32[32,4,128]{2,1,0:T(4,128)S(1)} custom-call(s32[1,2048]{1,0:T(1,128)S(1)} %bitcast.7, s32[2,2048]{1,0:T(2,128)S(1)} %copy-done.1, f32[2,2048]{1,0:T(2,128)S(1)} %copy-done.2), custom_call_target="tpu_custom_call" | custom-call | tf_op jit(solution)/shard_map/pack/pallas_call | solution.py:473
  13.7 0.0 copy-start.4
  13.7 0.6 %copy-done.4 = s32[4]{0:T(128)S(1)} copy-done((s32[4]{0:T(128)S(1)}, s32[4]{0:T(128)}, u32[]{:S(2)}) %copy-start.4) | copy-done | bytes 40
  14.4 0.0 copy-start
  14.4 0.9 %copy-done = f32[2,2,64,64]{3,2,1,0:T(8,128)S(1)} copy-done((f32[2,2,64,64]{3,2,1,0:T(8,128)S(1)}, f32[2,2,64,64]{3,2,1,0:T(8,128)}, u32[]{:S(2)}) %copy-start) | copy-done | bytes 65560
  15.3 39.7 %butterfly.1 = f32[2,64,1024]{2,1,0:T(8,128)S(1)} custom-call(s32[4]{0:T(128)S(1)} %copy-done.4, f32[16,4,256]{2,1,0:T(4,128)S(1)} %bitcast.6, f32[2,2,64,64]{3,2,1,0:T(8,128)S(1)} %copy-done), custom_call_target="tpu_custom_call" | custom-call | tf_op jit(solution)/shard_map/butterfly/pallas_call | solution.py:497
  55.0 0.8 %copy.7 = f32[2,64,1024]{2,1,0:T(8,128)} copy(f32[2,64,1024]{2,1,0:T(8,128)S(1)} %butterfly.1) | data formatting | bytes 1048576
Async XLA Ops:
  0.0 0.7 %copy-start.1 = (s32[2,2048]{1,0:T(2,128)S(1)}, s32[2,2048]{1,0:T(2,128)}, u32[]{:S(2)}) copy-start(s32[2,2048]{1,0:T(2,128)} %offset_hbm.1) | copy-start | bytes 49156
  0.7 0.7 %copy-start.2 = (f32[2,2048]{1,0:T(2,128)S(1)}, f32[2,2048]{1,0:T(2,128)}, u32[]{:S(2)}) copy-start(f32[2,2048]{1,0:T(2,128)} %value_hbm.1) | copy-start | bytes 49156
  1.4 0.7 %copy-start.3 = (s32[2048,1]{0,1:T(1,128)S(1)}, s32[2048,1]{0,1:T(1,128)}, u32[]{:S(2)}) copy-start(s32[2048,1]{0,1:T(1,128)} %param.5) | copy-start | bytes 24580
  13.7 0.7 %copy-start.4 = (s32[4]{0:T(128)S(1)}, s32[4]{0:T(128)}, u32[]{:S(2)}) copy-start(s32[4]{0:T(128)} %coef_ref.1) | copy-start | bytes 52
  14.4 0.9 %copy-start = (f32[2,2,64,64]{3,2,1,0:T(8,128)S(1)}, f32[2,2,64,64]{3,2,1,0:T(8,128)}, u32[]{:S(2)}) copy-start(f32[2,2,64,64]{3,2,1,0:T(8,128)} %constant.2.clone.merge_ref) | copy-start | bytes 196612
